TPU v7x, 32 devices: a whole 2x2x4 slice. The times are simulated.
32 devices in a mesh: gx: 4 (over z), gy: 4 (over y, x), gz: 2 (over core).
Axes of the slice: x: 2, y: 2, z: 4, core: 2. Of those that a mesh axis runs over, the one named last changes fastest.
Arguments:
- distribution: bfloat16 [8, 32, 16, 12, 512], P('gx', 'gy', 'gz'), may hold values from 0.019897461 to 1
- block_ids: int32 [8, 32, 16, 12], P('gx', 'gy', 'gz'), may hold values from 0 to 215, as said below
- cell_counts: int32 [8, 32, 16], P('gx', 'gy', 'gz'), may hold values from 6 to 12
- owner: int32 [8, 32, 16], P('gx', 'gy', 'gz'), may hold values from 0 to 7, as said below
- restitution: bfloat16 [8, 32, 16], P('gx', 'gy', 'gz'), may hold values from 0.5 to 0.94921875
Outputs:
- moved_distribution: bfloat16 [4, 1024, 12, 512], P('gy', ('gx', 'gz'))
- moved_ids: int32 [4, 1024, 12], P('gy', ('gx', 'gz'))
- moved_counts: int32 [4, 1024], P('gy', ('gx', 'gz'))
Inputs may be any that keep to these rules, and one draw needn't show every extreme that they name: `block_ids`: the 12 numbers of one cell are distinct block numbers. `owner`: owner g means the device of the cell's gy row with gx index g // 2 and gz index g % 2. Each device sends exactly 16 of its cells to each of the 8 devices of its gy row (itself included), and each device owns exactly 128 cells afterwards.
All inputs are finite; a program needn't handle non-finite values.
Results may differ from a plain program's by a relative error of at most 0.001.
The roundings to bfloat16 on the way count: a program that leaves them out, or rounds other values in their place, can miss the bound.
Values may be sent and summed in bfloat16 or wider, within the bound.
A program may use at most 64 MiB of HBM per device.

v0:
```python
import math

import jax
import jax.numpy as jnp
from jax import lax
from jax.sharding import PartitionSpec as P

NV1 = 48
BLK = 8
MAXB = 12


STEP_COEFF = 0.6
IMPACT_KIND = 0.02


def extended(value, sides, width):
    for axis, dim in sides:
        peers, length = (lax.axis_size(axis), value.shape[dim])
        up = [(i, (i + 1) % peers) for i in range(peers)]
        down = [(j, i) for i, j in up]
        last = lax.slice_in_dim(value, length - width, length, axis=dim)
        first = lax.slice_in_dim(value, 0, width, axis=dim)
        before = lax.ppermute(last, axis, up)
        after = lax.ppermute(first, axis, down)
        value = jnp.concatenate([before, value, after], axis=dim)
    return value


def inner_offsets():
    velocity_index = jnp.arange(BLK**3, dtype=jnp.int32)
    coords = jnp.stack(
        [velocity_index // (BLK * BLK), velocity_index // BLK % BLK, velocity_index % BLK]
    )
    return coords.astype(jnp.float32) - (BLK - 1) / 2.0


def block_centers(ids):
    blocks_edge = NV1 // BLK
    coords = jnp.stack(
        [ids // (blocks_edge * blocks_edge), ids // blocks_edge % blocks_edge, ids % blocks_edge]
    )
    return coords.astype(jnp.float32) * BLK + (BLK - 1) / 2.0 - (NV1 - 1) / 2.0


def neighbor_values(own_ids, other_ids, other_values):
    matches = (
        (own_ids[..., :, None] == other_ids[..., None, :]) & (own_ids[..., :, None] >= 0)
    ).astype(jnp.bfloat16)
    return jnp.einsum(
        "abcst,abctj->abcsj", matches, other_values, preferred_element_type=jnp.float32
    )


def relax(read, raw_ids, live_mask, coefficient):
    inner_offset = inner_offsets()
    centers = block_centers(raw_ids)
    tile_span = inner_offset.shape[1]
    squares = jnp.sum(inner_offset * inner_offset, axis=0)
    weights_table = jnp.concatenate(
        [jnp.ones((1, tile_span), jnp.float32), inner_offset, squares[None]], axis=0
    ).T.astype(jnp.bfloat16)
    leading = read.shape[:-1]
    block_sums = jnp.dot(
        read.reshape(-1, tile_span), weights_table, preferred_element_type=jnp.float32
    ).reshape(leading + (5,))
    block_mass = block_sums[..., 0]
    particle_count_field = jnp.sum(block_mass, axis=-1)
    momentum = [
        jnp.sum(block_mass * centers[k] + block_sums[..., 1 + k], axis=-1) for k in range(3)
    ]
    center_sq = centers[0] * centers[0] + centers[1] * centers[1] + centers[2] * centers[2]
    cross = (
        centers[0] * block_sums[..., 1]
        + centers[1] * block_sums[..., 2]
        + centers[2] * block_sums[..., 3]
    )
    motion_work_sum = jnp.sum(block_mass * center_sq + 2.0 * cross + block_sums[..., 4], axis=-1)
    average_drift = [momentum[k] / particle_count_field for k in range(3)]
    thermal_spread = (
        motion_work_sum / particle_count_field
        - (
            average_drift[0] * average_drift[0]
            + average_drift[1] * average_drift[1]
            + average_drift[2] * average_drift[2]
        )
    ) / 3.0
    return_parcels_home = coefficient.astype(jnp.float32)
    destination_holder = (
        thermal_spread * (1.0 + return_parcels_home) * (1.0 + return_parcels_home) / 4.0
    )
    equilibration_frequency = 1.0 - jnp.exp(
        -IMPACT_KIND * (particle_count_field / tile_span) * jnp.sqrt(thermal_spread)
    )
    distance = jnp.zeros(read.shape, jnp.float32)
    for k in range(3):
        offset_k = centers[k][..., None] + inner_offset[k] - average_drift[k][..., None, None]
        distance = distance + offset_k * offset_k
    scale = particle_count_field / (2.0 * math.pi * destination_holder) ** 1.5
    maxwellian = scale[..., None, None] * jnp.exp(
        -distance / (2.0 * destination_holder[..., None, None])
    )
    stream_vals = read.astype(jnp.float32)
    relaxed = (
        stream_vals + equilibration_frequency[..., None, None] * (maxwellian - stream_vals)
    ) * live_mask[..., None]
    return relaxed.astype(jnp.bfloat16)


def carry_cells(outgoing, metadata):
    return (
        lax.all_to_all(outgoing, ("gx", "gz"), split_axis=0, concat_axis=0, tiled=True),
        lax.all_to_all(metadata, ("gx", "gz"), split_axis=0, concat_axis=0, tiled=True),
    )


def on_device(distribution, block_ids, cell_counts, owner, restitution):
    size_x, size_y, size_z = cell_counts.shape
    slot_index = jnp.arange(MAXB, dtype=jnp.int32)
    live = slot_index < cell_counts[..., None]
    listed = jnp.where(live, block_ids, -1)
    padded = extended(distribution, (("gx", 0), ("gy", 1), ("gz", 2)), 1)
    padded_ids = extended(listed, (("gx", 0), ("gy", 1), ("gz", 2)), 1)
    neighbours = [
        (
            padded[:-2, 1:-1, 1:-1],
            padded_ids[:-2, 1:-1, 1:-1],
            padded[2:, 1:-1, 1:-1],
            padded_ids[2:, 1:-1, 1:-1],
        ),
        (
            padded[1:-1, :-2, 1:-1],
            padded_ids[1:-1, :-2, 1:-1],
            padded[1:-1, 2:, 1:-1],
            padded_ids[1:-1, 2:, 1:-1],
        ),
        (
            padded[1:-1, 1:-1, :-2],
            padded_ids[1:-1, 1:-1, :-2],
            padded[1:-1, 1:-1, 2:],
            padded_ids[1:-1, 1:-1, 2:],
        ),
    ]
    inner_offset = inner_offsets()
    centers = block_centers(block_ids)
    center_value = distribution.astype(jnp.float32)
    flux_sum = jnp.zeros(center_value.shape, jnp.float32)
    lam = STEP_COEFF / (NV1 - 1)
    for direction in range(3):
        lower_vals, lower_ids, upper_vals, upper_ids = neighbours[direction]
        velocity = centers[direction][..., None] + inner_offset[direction]
        from_lower = neighbor_values(listed, lower_ids, lower_vals)
        from_upper = neighbor_values(listed, upper_ids, upper_vals)
        flux_sum = (
            flux_sum
            + jnp.maximum(velocity, 0.0) * (center_value - from_lower)
            + jnp.minimum(velocity, 0.0) * (from_upper - center_value)
        )
    live_mask = live.astype(jnp.float32)
    read = ((center_value - lam * flux_sum) * live_mask[..., None]).astype(jnp.bfloat16)
    cell_total = size_x * size_y * size_z
    count_x = lax.axis_size("gx")
    count_z = lax.axis_size("gz")
    group_size = count_x * count_z
    capacity = cell_total // group_size
    id_columns = block_ids.reshape(cell_total, MAXB).astype(jnp.bfloat16)
    count_column = cell_counts.reshape(cell_total, 1).astype(jnp.bfloat16)
    payload = relax(read, block_ids, live_mask, restitution)
    metadata = jnp.concatenate([id_columns, count_column], axis=1)
    payload_rows = payload.reshape(cell_total, -1)
    row_width = payload_rows.shape[1]
    owners = owner.reshape(cell_total)
    onehot = (owners[:, None] == jnp.arange(group_size, dtype=jnp.int32)[None, :]).astype(jnp.int32)
    rank_within = jnp.sum((jnp.cumsum(onehot, axis=0) - onehot) * onehot, axis=1)
    positions = owners * capacity + rank_within
    outgoing = (
        jnp.zeros((group_size * capacity, row_width), jnp.bfloat16).at[positions].set(payload_rows)
    )
    outgoing_meta = (
        jnp.zeros((group_size * capacity, metadata.shape[1]), jnp.bfloat16)
        .at[positions]
        .set(metadata)
    )
    received, received_meta = carry_cells(outgoing, outgoing_meta)
    valid_slot = received_meta[:, MAXB] > 0
    targets = jnp.where(valid_slot, jnp.cumsum(valid_slot.astype(jnp.int32)) - 1, cell_total)
    placed = jnp.zeros((cell_total, row_width), jnp.bfloat16).at[targets].set(received, mode="drop")
    placed_meta = (
        jnp.zeros((cell_total, received_meta.shape[1]), jnp.bfloat16)
        .at[targets]
        .set(received_meta, mode="drop")
    )
    moved_ids = placed_meta[:, :MAXB].astype(jnp.int32)
    moved_counts = placed_meta[:, MAXB].astype(jnp.int32)
    placed_cells = placed.reshape(cell_total, MAXB, -1)
    return (
        placed_cells.reshape(1, cell_total, MAXB, -1),
        moved_ids.reshape(1, cell_total, MAXB),
        moved_counts.reshape(1, cell_total),
    )


def solution(mesh):
    placed = (
        P("gx", "gy", "gz", None, None),
        P("gx", "gy", "gz", None),
        P("gx", "gy", "gz"),
        P("gx", "gy", "gz"),
        P("gx", "gy", "gz"),
    )
    return jax.shard_map(
        on_device,
        mesh=mesh,
        in_specs=placed,
        out_specs=(
            P("gy", ("gx", "gz"), None, None),
            P("gy", ("gx", "gz"), None),
            P("gy", ("gx", "gz")),
        ),
        check_vma=False,
    )
```

profile of v0, /device:TPU:0, one launch (start us, length us, event | category | flops | bytes accessed | tf_op | source)
XLA Modules:
  0.0 157.3 jit_solution(8730132587896184400)
XLA Ops:
  0.6 0.9 broadcast_compare_fusion
  1.6 3.1 %collective-permute-start = (s32[1,8,8,12]{3,2,1,0:T(8,128)S(1)}, s32[1,8,8,12]{3,2,1,0:T(8,128)S(1)}, u32[]{:S(2)}, u32[]{:S(2)}) collective-permute-start(s32[1,8,8,12]{3,2,1,0:T(8,128)S(1)} %get-tuple-element.57), channel_id=1, source_target_pairs={{0,8},{8,16},{16,24},{24,0},{1,9},{9,17},{17,25},{25,1},{2,10},{10... | collective-permute-start | bytes 9224 | tf_op jit(solution)/shard_map/ppermute | solution.py:24
  4.7 2.1 %collective-permute-start.2 = (s32[1,8,8,12]{3,2,1,0:T(8,128)S(1)}, s32[1,8,8,12]{3,2,1,0:T(8,128)S(1)}, u32[]{:S(2)}, u32[]{:S(2)}) collective-permute-start(s32[1,8,8,12]{3,2,1,0:T(8,128)S(1)} %get-tuple-element.58), channel_id=1, source_target_pairs={{8,0},{16,8},{24,16},{0,24},{9,1},{17,9},{25,17},{1,25},{10,2},{18... | collective-permute-start | bytes 9224 | tf_op jit(solution)/shard_map/ppermute | solution.py:25
  6.7 0.7 convert_element_type.82
  7.4 0.8 eq.44
  8.2 0.7 broadcast_multiply_fusion
  8.9 1.1 fusion.71
  10.0 0.1 convert_element_type.83
  10.1 0.1 mul.230
  10.2 0.1 fusion.79
  10.3 0.2 reduce_window_sum.18
  10.4 0.2 select_reduce_fusion
  10.6 0.1 copy.56
  10.8 0.1 copy.58
  11.0 0.1 fusion.75
  11.1 1.4 scatter_custom_fusion
  12.5 3.3 %all-to-all-start = ((bf16[8,16,13]{2,1,0:T(8,128)(2,1)}), bf16[8,16,13]{2,1,0:T(8,128)(2,1)S(1)}, u32[]{:S(2)}, u32[]{:S(2)}) async-start(bf16[8,16,13]{2,1,0:T(8,128)(2,1)} %bitcast.2), calls=%async_computation | async-start | bytes 65536 | tf_op jit(solution)/shard_map/all_to_all | solution.py:113
  15.9 1.5 fusion.106
  17.4 3.8 %collective-permute-start.3 = (bf16[1,8,8,12,512]{4,2,3,1,0:T(8,128)(2,1)S(1)}, bf16[1,8,8,12,512]{4,2,3,1,0:T(8,128)(2,1)S(1)}, u32[]{:S(2)}, u32[]{:S(2)}) collective-permute-start(bf16[1,8,8,12,512]{4,2,3,1,0:T(8,128)(2,1)S(1)} %get-tuple-element.29), channel_id=1, source_target_pairs={{8,0},{16,8},{24,16},{0,24},{9,1},{17,9},{25,17},{1,25},{10,2},{18... | collective-permute-start | bytes 2359304 | tf_op jit(solution)/shard_map/ppermute | solution.py:25
  21.3 1.7 %collective-permute-start.4 = (s32[4,1,8,12]{3,2,1,0:T(8,128)S(1)}, s32[4,1,8,12]{3,2,1,0:T(8,128)S(1)}, u32[]{:S(2)}, u32[]{:S(2)}) collective-permute-start(s32[4,1,8,12]{3,2,1,0:T(8,128)S(1)} %get-tuple-element.48), channel_id=1, source_target_pairs={{0,2},{2,4},{4,6},{6,0},{1,3},{3,5},{5,7},{7,1},{8,10},{10,12},{12... | collective-permute-start | bytes 4616 | tf_op jit(solution)/shard_map/ppermute | solution.py:24
  23.0 1.3 collective-permute-start.6
  24.3 1.7 %collective-permute-done.4 = s32[4,1,8,12]{3,2,1,0:T(8,128)S(1)} collective-permute-done((s32[4,1,8,12]{3,2,1,0:T(8,128)S(1)}, s32[4,1,8,12]{3,2,1,0:T(8,128)S(1)}, u32[]{:S(2)}, u32[]{:S(2)}) %collective-permute-start.4) | collective-permute-done | bytes 1568 | tf_op jit(solution)/shard_map/ppermute | solution.py:24
  26.0 0.7 collective-permute-done.6
  26.9 0.5 collective-permute-start.8
  27.4 0.7 collective-permute-done.10
  28.0 0.2 collective-permute-done.8
  28.2 27.9 %collective-permute-done.1 = bf16[1,8,8,12,512]{4,2,3,1,0:T(8,128)(2,1)S(1)} collective-permute-done((bf16[1,8,8,12,512]{4,2,3,1,0:T(8,128)(2,1)S(1)}, bf16[1,8,8,12,512]{4,2,3,1,0:T(8,128)(2,1)S(1)}, u32[]{:S(2)}, u32[]{:S(2)}) %collective-permute-start.1) | collective-permute-done | bytes 786464 | tf_op jit(solution)/shard_map/ppermute | solution.py:24
  56.1 0.3 fusion.107
  56.4 0.7 fusion.105
  57.2 0.4 fusion.108
  57.7 1.7 %collective-permute-start.5 = (bf16[4,1,8,12,512]{4,3,2,1,0:T(8,128)(2,1)S(1)}, bf16[4,1,8,12,512]{4,3,2,1,0:T(8,128)(2,1)S(1)}, u32[]{:S(2)}, u32[]{:S(2)}) collective-permute-start(bf16[4,1,8,12,512]{4,3,2,1,0:T(8,128)(2,1)S(1)} %get-tuple-element.25), channel_id=1, source_target_pairs={{0,2},{2,4},{4,6},{6,0},{1,3},{3,5},{5,7},{7,1},{8,10},{10,12},{12... | collective-permute-start | bytes 1179656 | tf_op jit(solution)/shard_map/ppermute | solution.py:24
  59.4 1.3 collective-permute-start.7
  60.6 2.2 %fusion.31 = f32[2,8,8,12,512]{4,3,2,1,0:T(8,128)S(1)} fusion(bf16[1,8,8,12,512]{4,3,2,1,0:T(8,128)(2,1)S(1)} %get-tuple-element.33, bf16[2,8,8,12,512]{4,3,2,1,0:T(8,128)(2,1)S(1)} %get-tuple-element.27, s32[2,8,8,12]{3,2,1,0:T(8,128)S(1)} %get-tuple-element.51, s32[2,8,8,12]{3,2,1,0:T(8,128)S(1)} %get-tuple-element.22, ...), kind=kOutput, calls=%fused_computation.63 | convolution fusion | flops 19697664 | bytes 5518848 | tf_op jit(solution)/shard_map/abcst,abctj->abcsj/dot_general | solution.py:50
  62.9 2.3 %fusion.33 = f32[2,8,8,12,512]{4,3,2,1,0:T(8,128)S(1)} fusion(bf16[2,8,8,12,512]{4,3,2,1,0:T(8,128)(2,1)S(1)} %get-tuple-element.27, bf16[1,8,8,12,512]{4,3,2,1,0:T(8,128)(2,1)S(1)} %get-tuple-element.31, s32[2,8,8,12]{3,2,1,0:T(8,128)S(1)} %get-tuple-element.50, s32[2,8,8,12]{3,2,1,0:T(8,128)S(1)} %get-tuple-element.22, ...), kind=kOutput, calls=%fused_computation.66 | convolution fusion | flops 19697664 | bytes 5518848 | tf_op jit(solution)/shard_map/abcst,abctj->abcsj/dot_general | solution.py:50
  65.2 8.3 %collective-permute-done.5 = bf16[4,1,8,12,512]{4,3,2,1,0:T(8,128)(2,1)S(1)} collective-permute-done((bf16[4,1,8,12,512]{4,3,2,1,0:T(8,128)(2,1)S(1)}, bf16[4,1,8,12,512]{4,3,2,1,0:T(8,128)(2,1)S(1)}, u32[]{:S(2)}, u32[]{:S(2)}) %collective-permute-start.5) | collective-permute-done | bytes 393248 | tf_op jit(solution)/shard_map/ppermute | solution.py:24
  73.5 9.7 %collective-permute-done.7 = bf16[4,1,8,12,512]{4,3,2,1,0:T(8,128)(2,1)S(1)} collective-permute-done((bf16[4,1,8,12,512]{4,3,2,1,0:T(8,128)(2,1)S(1)}, bf16[4,1,8,12,512]{4,3,2,1,0:T(8,128)(2,1)S(1)}, u32[]{:S(2)}, u32[]{:S(2)}) %collective-permute-start.7) | collective-permute-done | bytes 393248 | tf_op jit(solution)/shard_map/ppermute | solution.py:25
  83.2 0.2 pad_maximum_fusion.20
  83.4 0.4 copy.69
  83.8 0.4 copy.67
  84.3 0.5 collective-permute-start.11
  84.8 2.3 %fusion.27 = f32[2,8,8,12,512]{4,3,2,1,0:T(8,128)S(1)} fusion(bf16[4,1,8,12,512]{4,3,2,1,0:T(8,128)(2,1)S(1)} %collective-permute-done.7, bf16[4,8,8,12,512]{4,3,2,1,0:T(8,128)(2,1)S(1)} %get-tuple-element.34, s32[2,8,8,12]{3,2,1,0:T(8,128)S(1)} %get-tuple-element.52, s32[2,8,8,12]{3,2,1,0:T(8,128)S(1)} %get-tuple-element.22, ...), kind=kOutput, calls=%fused_computation.57 | convolution fusion | flops 19697664 | bytes 6698496 | tf_op jit(solution)/shard_map/abcst,abctj->abcsj/dot_general | solution.py:50
  87.0 2.3 %fusion.29 = f32[2,8,8,12,512]{4,3,2,1,0:T(8,128)S(1)} fusion(bf16[4,8,8,12,512]{4,3,2,1,0:T(8,128)(2,1)S(1)} %get-tuple-element.34, bf16[4,1,8,12,512]{4,3,2,1,0:T(8,128)(2,1)S(1)} %collective-permute-done.5, s32[2,8,8,12]{3,2,1,0:T(8,128)S(1)} %get-tuple-element.47, s32[2,8,8,12]{3,2,1,0:T(8,128)S(1)} %get-tuple-element.22, ...), kind=kOutput, calls=%fused_computation.60 | convolution fusion | flops 19697664 | bytes 6698496 | tf_op jit(solution)/shard_map/abcst,abctj->abcsj/dot_general | solution.py:50
  89.4 0.1 copy.68
  89.5 0.1 copy.70
  89.7 1.5 fusion.25
  91.2 7.1 %multiply_convert_fusion = bf16[2,8,8,12,512]{4,3,2,1,0:T(8,128)(2,1)S(1)} fusion(f32[2,8,8,12,512]{4,3,2,1,0:T(8,128)S(1)} %fusion.25, f32[2,8,8,12,512]{4,3,2,1,0:T(8,128)S(1)} %fusion.27, f32[2,8,8,12,512]{4,3,2,1,0:T(8,128)S(1)} %fusion.29, f32[2,8,8,12,512]{4,3,2,1,0:T(8,128)S(1)} %fusion.31, f32[2,8,8,12,512]{4,3,2,1,0:T(8,128)S(1)} %fusion.33, ...), kind=kOutput, calls=%fused_computation.46 | convolution fusion | flops 45649920 | bytes 23342592 | tf_op jit(solution)/shard_map/abcst,abctj->abcsj/dot_general | solution.py:50
  98.3 2.6 %fusion.87 = f32[2,8,8,12,5]{3,4,2,1,0:T(8,128)S(1)} fusion(bf16[2,8,8,12,512]{4,3,2,1,0:T(8,128)(2,1)S(1)} %multiply_convert_fusion, bf16[1,512]{1,0:T(2,128)(2,1)S(1)} %broadcast_in_dim.9, bf16[3,512]{1,0:T(4,128)(2,1)S(1)} %get-tuple-element.65, bf16[5]{0:T(256)(128)(2,1)S(1)} %pad.clone), kind=kOutput, calls=%fused_computation.181 | convolution fusion | flops 7879680 | bytes 1607690 | tf_op jit(solution)/shard_map/dot_general | solution.py:64
  100.9 0.3 fusion.109
  101.1 0.1 reduce_sum.68
  101.2 0.2 add_reduce_fusion.3
  101.5 3.9 %fusion.2 = bf16[2,8,8,12,512]{4,3,2,1,0:T(8,128)(2,1)S(1)} fusion(bf16[2,8,8,12,512]{4,3,2,1,0:T(8,128)(2,1)S(1)} %multiply_convert_fusion, f32[2,8,8]{2,1,0:T(8,128)S(1)} %get-tuple-element.60, f32[2,8,8]{2,1,0:T(8,128)S(1)} %get-tuple-element.20, f32[2,8,8]{2,1,0:T(8,128)S(1)} %get-tuple-element.19, f32[2,8,8]{2,1,0:T(8,128)S(1)} %get-tuple-element.18, ...), kind=kLoop, calls=%fused_computation.24 | loop fusion | flops 15728640 | bytes 3179520 | tf_op jit(solution)/shard_map/convert_element_type | solution.py:107
  105.4 1.0 copy.84
  106.4 3.9 %scatter_custom_fusion.1 = bf16[128,6144]{1,0:T(8,128)(2,1)} fusion(s32[128]{0:T(128)S(1)} %fusion.75, bf16[128,6144]{1,0:T(8,128)(2,1)S(1)} %bitcast.69, bf16[]{:T(256)} %constant.132.clone.1), kind=kCustom, calls=%fused_computation.82 | custom fusion | bytes 1572866 | tf_op jit(solution)/shard_map/scatter | solution.py:177
  110.3 3.6 %all-to-all-start.1 = ((bf16[8,16,6144]{2,1,0:T(8,128)(2,1)}), bf16[8,16,6144]{2,1,0:T(8,128)(2,1)S(1)}, u32[]{:S(2)}, u32[]{:S(2)}) async-start(bf16[8,16,6144]{2,1,0:T(8,128)(2,1)} %bitcast.20), calls=%async_computation.1 | async-start | bytes 3145728 | tf_op jit(solution)/shard_map/all_to_all | solution.py:112
  113.9 0.1 fusion.94
  114.0 0.2 reduce-window.4
  114.2 0.2 fusion.76
  114.4 1.1 scatter_custom_fusion.3
  115.5 0.7 copy.77
  116.2 0.7 convert_reduce_fusion
  116.9 34.8 %all-to-all-done.1 = bf16[8,16,6144]{2,1,0:T(8,128)(2,1)S(1)} async-done(((bf16[8,16,6144]{2,1,0:T(8,128)(2,1)}), bf16[8,16,6144]{2,1,0:T(8,128)(2,1)S(1)}, u32[]{:S(2)}, u32[]{:S(2)}) %all-to-all-start.1) | async-done | bytes 1572896 | tf_op jit(solution)/shard_map/all_to_all | solution.py:112
  151.7 3.1 %scatter_custom_fusion.2 = bf16[128,6144]{1,0:T(8,128)(2,1)S(1)} fusion(s32[128]{0:T(128)S(1)} %fusion.76, bf16[128,6144]{1,0:T(8,128)(2,1)S(1)} %bitcast.70, bf16[]{:T(256)} %constant.132.clone.1), kind=kCustom, calls=%fused_computation.80 | custom fusion | bytes 1572866 | tf_op jit(solution)/shard_map/scatter | solution.py:187
  154.8 0.9 copy.75
  155.7 1.6 copy.76
  (34 shorter events, 0.6 us)
Async XLA Ops:
  1.6 19.7 %collective-permute-start = (s32[1,8,8,12]{3,2,1,0:T(8,128)S(1)}, s32[1,8,8,12]{3,2,1,0:T(8,128)S(1)}, u32[]{:S(2)}, u32[]{:S(2)}) collective-permute-start(s32[1,8,8,12]{3,2,1,0:T(8,128)S(1)} %get-tuple-element.57), channel_id=1, source_target_pairs={{0,8},{8,16},{16,24},{24,0},{1,9},{9,17},{17,25},{25,1},{2,10},{10... | collective-permute-start | bytes 9224 | tf_op jit(solution)/shard_map/ppermute | solution.py:24
  4.7 16.6 %collective-permute-start.2 = (s32[1,8,8,12]{3,2,1,0:T(8,128)S(1)}, s32[1,8,8,12]{3,2,1,0:T(8,128)S(1)}, u32[]{:S(2)}, u32[]{:S(2)}) collective-permute-start(s32[1,8,8,12]{3,2,1,0:T(8,128)S(1)} %get-tuple-element.58), channel_id=1, source_target_pairs={{8,0},{16,8},{24,16},{0,24},{9,1},{17,9},{25,17},{1,25},{10,2},{18... | collective-permute-start | bytes 9224 | tf_op jit(solution)/shard_map/ppermute | solution.py:25
  10.6 45.8 %copy-start = (bf16[2,8,8,12,512]{4,2,3,1,0:T(8,128)(2,1)S(1)}, bf16[2,8,8,12,512]{4,2,3,1,0:T(8,128)(2,1)}, u32[]{:S(2)}) copy-start(bf16[2,8,8,12,512]{4,2,3,1,0:T(8,128)(2,1)} %param.5) | copy-start | bytes 4718596
  12.5 97.8 %all-to-all-start = ((bf16[8,16,13]{2,1,0:T(8,128)(2,1)}), bf16[8,16,13]{2,1,0:T(8,128)(2,1)S(1)}, u32[]{:S(2)}, u32[]{:S(2)}) async-start(bf16[8,16,13]{2,1,0:T(8,128)(2,1)} %bitcast.2), calls=%async_computation | async-start | bytes 65536 | tf_op jit(solution)/shard_map/all_to_all | solution.py:113
  17.4 39.8 %collective-permute-start.3 = (bf16[1,8,8,12,512]{4,2,3,1,0:T(8,128)(2,1)S(1)}, bf16[1,8,8,12,512]{4,2,3,1,0:T(8,128)(2,1)S(1)}, u32[]{:S(2)}, u32[]{:S(2)}) collective-permute-start(bf16[1,8,8,12,512]{4,2,3,1,0:T(8,128)(2,1)S(1)} %get-tuple-element.29), channel_id=1, source_target_pairs={{8,0},{16,8},{24,16},{0,24},{9,1},{17,9},{25,17},{1,25},{10,2},{18... | collective-permute-start | bytes 2359304 | tf_op jit(solution)/shard_map/ppermute | solution.py:25
  21.2 35.0 %collective-permute-start.1 = (bf16[1,8,8,12,512]{4,2,3,1,0:T(8,128)(2,1)S(1)}, bf16[1,8,8,12,512]{4,2,3,1,0:T(8,128)(2,1)S(1)}, u32[]{:S(2)}, u32[]{:S(2)}) collective-permute-start(bf16[1,8,8,12,512]{4,2,3,1,0:T(8,128)(2,1)S(1)} %get-tuple-element.30), channel_id=1, source_target_pairs={{0,8},{8,16},{16,24},{24,0},{1,9},{9,17},{17,25},{25,1},{2,10},{10... | collective-permute-start | bytes 2359304 | tf_op jit(solution)/shard_map/ppermute | solution.py:24
  21.3 4.7 %collective-permute-start.4 = (s32[4,1,8,12]{3,2,1,0:T(8,128)S(1)}, s32[4,1,8,12]{3,2,1,0:T(8,128)S(1)}, u32[]{:S(2)}, u32[]{:S(2)}) collective-permute-start(s32[4,1,8,12]{3,2,1,0:T(8,128)S(1)} %get-tuple-element.48), channel_id=1, source_target_pairs={{0,2},{2,4},{4,6},{6,0},{1,3},{3,5},{5,7},{7,1},{8,10},{10,12},{12... | collective-permute-start | bytes 4616 | tf_op jit(solution)/shard_map/ppermute | solution.py:24
  23.0 3.7 %collective-permute-start.6 = (s32[4,1,8,12]{3,2,1,0:T(8,128)S(1)}, s32[4,1,8,12]{3,2,1,0:T(8,128)S(1)}, u32[]{:S(2)}, u32[]{:S(2)}) collective-permute-start(s32[4,1,8,12]{3,2,1,0:T(8,128)S(1)} %get-tuple-element.49), channel_id=1, source_target_pairs={{2,0},{4,2},{6,4},{0,6},{3,1},{5,3},{7,5},{1,7},{10,8},{12,10},{14... | collective-permute-start | bytes 4616 | tf_op jit(solution)/shard_map/ppermute | solution.py:25
  26.8 1.3 collective-permute-start.10
  26.9 1.3 collective-permute-start.8
  57.7 15.8 %collective-permute-start.5 = (bf16[4,1,8,12,512]{4,3,2,1,0:T(8,128)(2,1)S(1)}, bf16[4,1,8,12,512]{4,3,2,1,0:T(8,128)(2,1)S(1)}, u32[]{:S(2)}, u32[]{:S(2)}) collective-permute-start(bf16[4,1,8,12,512]{4,3,2,1,0:T(8,128)(2,1)S(1)} %get-tuple-element.25), channel_id=1, source_target_pairs={{0,2},{2,4},{4,6},{6,0},{1,3},{3,5},{5,7},{7,1},{8,10},{10,12},{12... | collective-permute-start | bytes 1179656 | tf_op jit(solution)/shard_map/ppermute | solution.py:24
  59.4 23.8 %collective-permute-start.7 = (bf16[4,1,8,12,512]{4,3,2,1,0:T(8,128)(2,1)S(1)}, bf16[4,1,8,12,512]{4,3,2,1,0:T(8,128)(2,1)S(1)}, u32[]{:S(2)}, u32[]{:S(2)}) collective-permute-start(bf16[4,1,8,12,512]{4,3,2,1,0:T(8,128)(2,1)S(1)} %get-tuple-element.26), channel_id=1, source_target_pairs={{2,0},{4,2},{6,4},{0,6},{3,1},{5,3},{7,5},{1,7},{10,8},{12,10},{14... | collective-permute-start | bytes 1179656 | tf_op jit(solution)/shard_map/ppermute | solution.py:25
  84.2 5.2 %collective-permute-start.9 = (bf16[4,10,1,12,512]{4,0,3,2,1:T(4,128)(2,1)S(1)}, bf16[4,10,1,12,512]{4,0,3,2,1:T(4,128)(2,1)S(1)}, u32[]{:S(2)}, u32[]{:S(2)}) collective-permute-start(bf16[4,10,1,12,512]{4,0,3,2,1:T(4,128)(2,1)S(1)} %copy.67), channel_id=1, source_target_pairs={{0,1},{1,0},{2,3},{3,2},{4,5},{5,4},{6,7},{7,6},{8,9},{9,8},{10,11... | collective-permute-start | bytes 1474568 | tf_op jit(solution)/shard_map/ppermute | solution.py:24
  84.3 5.2 %collective-permute-start.11 = (bf16[4,10,1,12,512]{4,0,3,2,1:T(4,128)(2,1)S(1)}, bf16[4,10,1,12,512]{4,0,3,2,1:T(4,128)(2,1)S(1)}, u32[]{:S(2)}, u32[]{:S(2)}) collective-permute-start(bf16[4,10,1,12,512]{4,0,3,2,1:T(4,128)(2,1)S(1)} %copy.69), channel_id=1, source_target_pairs={{1,0},{0,1},{3,2},{2,3},{5,4},{4,5},{7,6},{6,7},{9,8},{8,9},{11,10... | collective-permute-start | bytes 1474568 | tf_op jit(solution)/shard_map/ppermute | solution.py:25
  89.6 1.5 copy-start.1
  91.2 10.2 %copy-start.2 = (bf16[2,8,8]{2,1,0:T(8,128)(2,1)S(1)}, bf16[2,8,8]{2,1,0:T(8,128)(2,1)}, u32[]{:S(2)}) copy-start(bf16[2,8,8]{2,1,0:T(8,128)(2,1)} %param.9) | copy-start | bytes 772
  110.3 41.3 %all-to-all-start.1 = ((bf16[8,16,6144]{2,1,0:T(8,128)(2,1)}), bf16[8,16,6144]{2,1,0:T(8,128)(2,1)S(1)}, u32[]{:S(2)}, u32[]{:S(2)}) async-start(bf16[8,16,6144]{2,1,0:T(8,128)(2,1)} %bitcast.20), calls=%async_computation.1 | async-start | bytes 3145728 | tf_op jit(solution)/shard_map/all_to_all | solution.py:112
where the time goes:
time: 158 us; the launch traced here: 157 us
  waiting for transfers between devices  84 us (53%)
  starting transfers between devices  23 us (15%)
  matrix products  20.3 us (13%)
  local copies, waits for them, and re-layouts  19.4 us (12%)
  other arithmetic  9.62 us (6%)
    ppermute x6, waiting for transfers between devices, extended(): before = lax.ppermute(last, axis, up)  38 us
    all_to_all x1, waiting for transfers between devices, carry_cells(): lax.all_to_all(outgoing, ('gx', 'gz'), split_axis=0, concat_axis=0, tiled...  34.8 us
    dot_general x6, matrix products, neighbor_values(): jnp.einsum('abcst,abctj->abcsj', matches, other_values, preferred_element...  17.7 us
    ppermute x6, waiting for transfers between devices, extended(): after = lax.ppermute(first, axis, down)  11.2 us
    ppermute x6, starting transfers between devices, extended(): after = lax.ppermute(first, axis, down)  9.01 us
    ppermute x6, starting transfers between devices, extended(): before = lax.ppermute(last, axis, up)  7.05 us
    scatter x2, local copies, waits for them, and re-layouts, on_device(): jnp.zeros((cell_total, row_width), jnp.bfloat16).at[targets]  4.02 us
    unnamed x10, local copies, waits for them, and re-layouts  4.02 us
  transfers between devices with their start and end apart: 14, of which 8 were waited for; matrix products, arithmetic and copies ran while one was open for 27% of the time, Pallas kernels for 0%

commit v1 on v0

v1 whole, which is shorter than its diff:
```python
import functools
import math

import jax
import jax.numpy as jnp
from jax import lax
from jax.experimental import pallas as pl
from jax.experimental.pallas import tpu as pltpu
from jax.sharding import PartitionSpec as P

NV1 = 48
BLK = 8
EDGE = NV1 // BLK
STEP_COEFF = 0.6
IMPACT_KIND = 0.02
ZPAD = 16


def weights():
    j = jnp.arange(BLK**3, dtype=jnp.int32)
    w = [c.astype(jnp.float32) - (BLK - 1) / 2.0 for c in (j // (BLK * BLK), j // BLK % BLK, j % BLK)]
    cols = [jnp.ones_like(w[0]), *w, w[0] * w[0] + w[1] * w[1] + w[2] * w[2]]
    return jnp.concatenate([jnp.broadcast_to(c[:, None], (BLK**3, 128)) for c in cols], axis=1).astype(jnp.bfloat16)


def column(slots, sz, ext_x, ext_y, own, zrows, xkeys, ykeys, zkeys, ids, coef, w_ref):
    rows = slots * sz
    shape = (rows, 128)
    listed = jnp.broadcast_to(ids, shape)
    live = listed >= 0
    z = lax.broadcasted_iota(jnp.int32, shape, 0) % sz
    bx = (listed * 1821) >> 16
    rem = listed - bx * (EDGE * EDGE)
    by = (rem * 10923) >> 16
    bz = rem - by * EDGE
    half = EDGE // 2

    def match(key, other):
        key = jnp.where(live, key, -5)[:, :1]
        return jnp.where(key == other, 1.0, 0.0).astype(jnp.bfloat16)

    mx = match(listed + 256 * z + jnp.where(bx >= half, 0, 4096), xkeys)
    my = match(listed + 256 * z + jnp.where(by >= half, 0, 4096), ykeys)
    mz = match(listed + 256 * jnp.where(bz >= half, z, z + 2), zkeys)
    dot = functools.partial(jnp.dot, preferred_element_type=jnp.float32)
    gx = dot(mx, jnp.concatenate(ext_x, axis=0))
    gy = dot(my, jnp.concatenate(ext_y, axis=0))
    gz = dot(mz, jnp.concatenate([own, zrows], axis=0))

    offset = (BLK - 1) / 2.0 - (NV1 - 1) / 2.0
    c = [b.astype(jnp.float32) * BLK + offset for b in (bx, by, bz)]
    lane = lax.broadcasted_iota(jnp.int32, (1, 128), 1)
    mid = (BLK - 1) / 2.0
    wx = [(lane // 64 + 2 * t).astype(jnp.float32) - mid for t in range(4)]
    wy = (lane // BLK % BLK).astype(jnp.float32) - mid
    wz = (lane % BLK).astype(jnp.float32) - mid
    vy, vz = jnp.abs(c[1] + wy), jnp.abs(c[2] + wz)
    lam = STEP_COEFF / (NV1 - 1)
    reads = []
    for t in range(4):
        cut = slice(128 * t, 128 * (t + 1))
        f = own[:, cut].astype(jnp.float32)
        flux = jnp.abs(c[0] + wx[t]) * (f - gx[:, cut]) + vy * (f - gy[:, cut]) + vz * (f - gz[:, cut])
        reads.append(jnp.where(live, f - lam * flux, 0.0).astype(jnp.bfloat16))
    sums = dot(reads[0], w_ref[0:128, :])
    for t in range(1, 4):
        sums = sums + dot(reads[t], w_ref[128 * t : 128 * (t + 1), :])
    s = [sums[:, 128 * k : 128 * (k + 1)] for k in range(5)]

    def per_cell(a):
        return jnp.sum(a.reshape(slots, sz, 128), axis=0)

    mass = per_cell(s[0])
    momentum = [per_cell(s[0] * c[k] + s[1 + k]) for k in range(3)]
    sq = c[0] * c[0] + c[1] * c[1] + c[2] * c[2]
    cross = c[0] * s[1] + c[1] * s[2] + c[2] * s[3]
    energy = per_cell(s[0] * sq + 2.0 * cross + s[4])
    u = [m / mass for m in momentum]
    temperature = (energy / mass - (u[0] * u[0] + u[1] * u[1] + u[2] * u[2])) / 3.0
    target = temperature * (1.0 + coef) * (1.0 + coef) / 4.0
    rate = 1.0 - jnp.exp(-IMPACT_KIND * (mass / BLK**3) * jnp.sqrt(temperature))
    area = 2.0 * math.pi * target
    scale = mass / (area * jnp.sqrt(area))
    inv = -0.5 / target

    cube = (slots, sz, 128)
    a = [c[k].reshape(cube) - u[k][None] for k in range(3)]
    oy, oz = a[1] + wy[None], a[2] + wz[None]
    q = oy * oy + oz * oz
    live3 = listed.reshape(cube) >= 0
    outs = []
    for t in range(4):
        ox = a[0] + wx[t][None]
        maxwellian = scale[None] * jnp.exp((ox * ox + q) * inv[None])
        r = reads[t].astype(jnp.float32).reshape(cube)
        outs.append(jnp.where(live3, r + rate[None] * (maxwellian - r), 0.0))
    return outs


def compute_kernel(sizes, ext, zh, xk, yk, zk, ids, coef, w_ref, pos, out, pay):
    cx, cy, sz, slots, groups, cap = sizes

    def body(n, carry):
        x, y = n // cy, n % cy
        outs = column(
            slots, sz,
            [ext[x, y + 1], ext[x + 2, y + 1]],
            [ext[x + 1, y], ext[x + 1, y + 2]],
            ext[x + 1, y + 1], zh[n], xk[n], yk[n], zk[n], ids[n], coef[n], w_ref,
        )
        for t in range(4):
            pay[:, pl.ds(pl.multiple_of(n * sz, sz), sz), 128 * t : 128 * (t + 1)] = outs[t]
        return carry

    lax.fori_loop(0, cx * cy, body, 0)
    cells = cx * cy * sz
    perm = jnp.where(lax.broadcasted_iota(jnp.int32, (cells, cells), 0) == pos[...], 1.0, 0.0).astype(jnp.bfloat16)

    def send(s, carry):
        rows = jnp.dot(perm, pay[s].astype(jnp.bfloat16), preferred_element_type=jnp.float32)
        for g in range(groups):
            out[g, s] = rows[g * cap : (g + 1) * cap].astype(jnp.bfloat16)
        return carry

    lax.fori_loop(0, slots, send, 0)


def shifted(value, axis, step):
    peers = lax.axis_size(axis)
    return lax.ppermute(value, axis, [(i, (i + step) % peers) for i in range(peers)])


def on_device(distribution, block_ids, cell_counts, owner, restitution):
    cx, cy, sz, slots, vb = distribution.shape
    cells, rows = cx * cy * sz, slots * sz
    groups = lax.axis_size("gx") * lax.axis_size("gz")
    cap = cells // groups
    live = jnp.arange(slots, dtype=jnp.int32) < cell_counts[..., None]
    listed = jnp.where(live, block_ids, -1).transpose(0, 1, 3, 2)
    f = distribution.transpose(0, 1, 3, 2, 4)

    xlo, xhi = shifted(f[-1:], "gx", 1), shifted(f[:1], "gx", -1)
    ylo, yhi = shifted(f[:, -1:], "gy", 1), shifted(f[:, :1], "gy", -1)
    zlo, zhi = shifted(f[:, :, :, -1], "gz", 1), shifted(f[:, :, :, 0], "gz", -1)
    ixlo, ixhi = shifted(listed[-1:], "gx", 1), shifted(listed[:1], "gx", -1)
    iylo, iyhi = shifted(listed[:, -1:], "gy", 1), shifted(listed[:, :1], "gy", -1)
    izlo, izhi = shifted(listed[..., -1], "gz", 1), shifted(listed[..., 0], "gz", -1)

    middle = jnp.concatenate([ylo, f, yhi], axis=1)
    wide = ((0, 0), (1, 1), (0, 0), (0, 0), (0, 0))
    ext = jnp.concatenate([jnp.pad(xlo, wide), middle, jnp.pad(xhi, wide)], axis=0)
    ext = ext.reshape(cx + 2, cy + 2, rows, vb)
    pad = ((0, 0), (0, 0), (0, ZPAD - slots), (0, 0))
    zh = jnp.concatenate([jnp.pad(zlo, pad), jnp.pad(zhi, pad)], axis=2).reshape(cx * cy, 2 * ZPAD, vb)

    keyed = lambda ids: (ids + 256 * jnp.arange(sz, dtype=jnp.int32)).reshape(ids.shape[0], ids.shape[1], rows)
    xk = keyed(jnp.concatenate([ixlo, listed, ixhi], axis=0))
    xk = jnp.concatenate([xk[:-2], xk[2:] + 4096], axis=-1).reshape(cx * cy, 1, 2 * rows)
    yk = keyed(jnp.concatenate([iylo, listed, iyhi], axis=1))
    yk = jnp.concatenate([yk[:, :-2], yk[:, 2:] + 4096], axis=-1).reshape(cx * cy, 1, 2 * rows)
    none = ((0, 0), (0, 0), (0, ZPAD - slots))
    zk = jnp.concatenate(
        [
            keyed(listed) + 256,
            jnp.pad(izlo, none, constant_values=-9),
            jnp.pad(izhi + 256 * (sz + 1), none, constant_values=-9),
        ],
        axis=-1,
    ).reshape(cx * cy, 1, rows + 2 * ZPAD)
    ids = listed.reshape(cx * cy, rows, 1)
    coef = jnp.broadcast_to(restitution.astype(jnp.float32).reshape(cx * cy, sz, 1), (cx * cy, sz, 128))

    owners = owner.reshape(cells)
    order = jnp.arange(cells, dtype=jnp.int32)
    same = (owners[:, None] == owners[None, :]) & (order[:, None] < order[None, :])
    pos = owners * cap + jnp.sum(same.astype(jnp.int32), axis=0)

    meta = jnp.concatenate([block_ids.reshape(cells, slots), cell_counts.reshape(cells, 1)], axis=1)
    onehot = (order[:, None] == pos[None, :]).astype(jnp.bfloat16)
    meta = jnp.dot(onehot, meta.astype(jnp.bfloat16), preferred_element_type=jnp.float32).astype(jnp.bfloat16)
    meta = lax.all_to_all(meta, ("gx", "gz"), split_axis=0, concat_axis=0, tiled=True).astype(jnp.int32)

    sizes = (cx, cy, sz, slots, groups, cap)
    outgoing = pl.pallas_call(
        functools.partial(compute_kernel, sizes),
        out_shape=jax.ShapeDtypeStruct((groups, slots, cap, vb), jnp.bfloat16),
        in_specs=[pl.BlockSpec(memory_space=pltpu.VMEM)] * 9,
        out_specs=pl.BlockSpec(memory_space=pltpu.VMEM),
        scratch_shapes=[pltpu.VMEM((slots, cells, vb), jnp.float32)],
        compiler_params=pltpu.CompilerParams(vmem_limit_bytes=40 << 20),
        name="transport_relax",
    )(ext, zh, xk, yk, zk, ids, coef, weights(), pos.reshape(1, cells))
    received = lax.all_to_all(outgoing, ("gx", "gz"), split_axis=0, concat_axis=0, tiled=True)
    moved = received.transpose(0, 2, 1, 3).reshape(1, cells, slots, vb)
    return moved, meta[:, :slots].reshape(1, cells, slots), meta[:, slots].reshape(1, cells)


def solution(mesh):
    placed = (
        P("gx", "gy", "gz", None, None),
        P("gx", "gy", "gz", None),
        P("gx", "gy", "gz"),
        P("gx", "gy", "gz"),
        P("gx", "gy", "gz"),
    )
    return jax.shard_map(
        on_device,
        mesh=mesh,
        in_specs=placed,
        out_specs=(
            P("gy", ("gx", "gz"), None, None),
            P("gy", ("gx", "gz"), None),
            P("gy", ("gx", "gz")),
        ),
        check_vma=False,
    )
```

time: 158 us -> 126 us (0.80)
  waiting for transfers between devices: 84 us -> 63.3 us
  matrix products: 20.3 us -> 0.17 us
  Pallas kernels: 0 us -> 14.8 us
  local copies, waits for them, and re-layouts: 19.4 us -> 14.5 us
  other arithmetic: 9.62 us -> 6.27 us
  starting transfers between devices: 23 us -> 25.4 us
    ppermute x12, waiting for transfers between devices: 49.2 us -> 26.7 us  [shifted(): lax.ppermute(value, axis, [(i, (i + step) % peers) for i in range(peers)])]
    dot_general x7 -> x1, matrix products: 20.3 us -> 0.17 us  [on_device(): jnp.dot(onehot, meta.astype(jnp.bfloat16), preferred_element_type=jnp.flo...]
    pallas_call x0 -> x1, Pallas kernels: none -> 14.8 us  [on_device(): pl.pallas_call(functools.partial(compute_kernel, sizes), out_shape=jax.Sh...]
    scatter x5 -> x0, local copies, waits for them, and re-layouts: 10.5 us -> none  [the longest x2 4.02 us: on_device(): jnp.zeros((cell_total, row_width), jnp.bfloat16).at[targets]]
    concatenate x5, other arithmetic: 0.3 us -> 5.88 us  [the longest x1 4.67 us: on_device(): jnp.concatenate([jnp.pad(xlo, wide), middle, jnp.pad(xhi, wide)], axis=0)]
    convert_element_type x5 -> x1, other arithmetic: 5.44 us -> 0.01 us  [on_device(): lax.all_to_all(meta, ('gx', 'gz'), split_axis=0, concat_axis=0, tiled=True)]
    all_to_all x2, starting transfers between devices: 6.92 us -> 10.1 us  [the longest x1 5.1 us: on_device(): lax.all_to_all(meta, ('gx', 'gz'), split_axis=0, concat_axis=0, tiled=True)]
    concatenate x2 -> x7, local copies, waits for them, and re-layouts: 0.14 us -> 2.94 us  [the longest x1 2.23 us: on_device(): jnp.concatenate([jnp.pad(xlo, wide), middle, jnp.pad(xhi, wide)], axis=0)]
  transfers between devices with their start and end apart: 14 -> 14, of which waited for: 8 -> 6; matrix products, arithmetic and copies ran while one was open for 27% -> 13% of each run, Pallas kernels for 0% -> 12%
where the time goes in v1:
time: 126 us; the launch traced here: 125 us
  waiting for transfers between devices  63.3 us (50%)
  starting transfers between devices  25.4 us (20%)
  Pallas kernels  14.8 us (12%)
  local copies, waits for them, and re-layouts  14.5 us (12%)
  other arithmetic  6.27 us (5%)
    all_to_all x1, waiting for transfers between devices, on_device(): lax.all_to_all(outgoing, ('gx', 'gz'), split_axis=0, concat_axis=0, tiled...  36.6 us
    ppermute x12, waiting for transfers between devices, shifted(): lax.ppermute(value, axis, [(i, (i + step) % peers) for i in range(peers)])  26.7 us
    ppermute x12, starting transfers between devices, shifted(): lax.ppermute(value, axis, [(i, (i + step) % peers) for i in range(peers)])  15.2 us
    pallas_call x1, Pallas kernels, on_device(): pl.pallas_call(functools.partial(compute_kernel, sizes), out_shape=jax.Sh...  14.8 us
    all_to_all x1, starting transfers between devices, on_device(): lax.all_to_all(meta, ('gx', 'gz'), split_axis=0, concat_axis=0, tiled=True)  5.1 us
    all_to_all x1, starting transfers between devices, on_device(): lax.all_to_all(outgoing, ('gx', 'gz'), split_axis=0, concat_axis=0, tiled...  5.05 us
    concatenate x1, other arithmetic, on_device(): jnp.concatenate([jnp.pad(xlo, wide), middle, jnp.pad(xhi, wide)], axis=0)  4.67 us
    unnamed x15, local copies, waits for them, and re-layouts  3.52 us
  transfers between devices with their start and end apart: 14, of which 6 were waited for; matrix products, arithmetic and copies ran while one was open for 13% of the time, Pallas kernels for 12%

profile of v1, /device:TPU:0, one launch (start us, length us, event | category | flops | bytes accessed | tf_op | source)
XLA Modules:
  0.0 125.4 jit_solution(15965018509475121320)
XLA Ops:
  0.7 2.3 %copy.140 = bf16[2,8,8,12,512]{4,1,3,0,2:T(8,128)(2,1)S(1)} copy(bf16[2,8,8,12,512]{4,2,3,1,0:T(8,128)(2,1)} %param.5) | data formatting | bytes 3145728 | tf_op args[0]
  3.0 1.3 %fusion.33 = (bf16[1,8,12,8,512]{4,1,2,0,3:T(8,128)(2,1)}, bf16[1,8,12,8,512]{4,1,2,0,3:T(8,128)(2,1)}) fusion(bf16[2,8,12,8,512]{4,1,2,0,3:T(8,128)(2,1)S(1)} %bitcast.46), kind=kLoop, calls=%fused_computation.86 | loop fusion | bytes 3145728 | tf_op jit(solution)/shard_map/slice | solution.py:142
  4.3 5.0 %collective-permute-start.3 = (bf16[1,8,12,8,512]{4,1,2,0,3:T(8,128)(2,1)}, bf16[1,8,12,8,512]{4,1,2,0,3:T(8,128)(2,1)}, u32[]{:S(2)}, u32[]{:S(2)}) collective-permute-start(bf16[1,8,12,8,512]{4,1,2,0,3:T(8,128)(2,1)} %get-tuple-element.19), channel_id=1, source_target_pairs={{0,24},{8,0},{16,8},{24,16},{1,25},{9,1},{17,9},{25,17},{2,26},{10... | collective-permute-start | bytes 2359304 | tf_op jit(solution)/shard_map/ppermute | solution.py:130
  9.3 1.5 %fusion.32 = (bf16[2,1,12,8,512]{4,1,2,0,3:T(2,128)(2,1)}, bf16[2,1,12,8,512]{4,1,2,0,3:T(2,128)(2,1)}) fusion(bf16[2,8,12,8,512]{4,1,2,0,3:T(8,128)(2,1)S(1)} %bitcast.47), kind=kLoop, calls=%fused_computation.85 | loop fusion | bytes 786432 | tf_op jit(solution)/shard_map/slice | solution.py:143
  10.9 2.4 %collective-permute-start.2 = (bf16[2,1,12,8,512]{4,1,2,0,3:T(2,128)(2,1)}, bf16[2,1,12,8,512]{4,1,2,0,3:T(2,128)(2,1)}, u32[]{:S(2)}, u32[]{:S(2)}) collective-permute-start(bf16[2,1,12,8,512]{4,1,2,0,3:T(2,128)(2,1)} %get-tuple-element.17), channel_id=1, source_target_pairs={{0,6},{2,0},{4,2},{6,4},{1,7},{3,1},{5,3},{7,5},{8,14},{10,8},{12,... | collective-permute-start | bytes 589832 | tf_op jit(solution)/shard_map/ppermute | solution.py:130
  13.3 0.1 copy.109
  13.4 0.1 add_add_fusion.1
  13.5 0.6 collective-permute-start.9
  14.1 1.5 %collective-permute-start.8 = (s32[2,1,12,8]{2,1,0,3:T(1,128)S(1)}, s32[2,1,12,8]{2,1,0,3:T(1,128)S(1)}, u32[]{:S(2)}, u32[]{:S(2)}) collective-permute-start(s32[2,1,12,8]{2,1,0,3:T(1,128)S(1)} %get-tuple-element.24), channel_id=1, source_target_pairs={{0,2},{2,4},{4,6},{6,0},{1,3},{3,5},{5,7},{7,1},{8,10},{10,12},{12... | collective-permute-start | bytes 2312 | tf_op jit(solution)/shard_map/ppermute | solution.py:130
  15.6 0.1 eq.14
  15.7 0.1 convert_reduce_fusion
  15.8 0.1 reshape.163
  15.9 0.1 copy.131
  16.0 0.2 convolution_convert_fusion
  16.1 0.1 all_to_all.10
  16.3 0.6 copy.127
  16.9 5.1 %all-to-all-start.1 = ((bf16[8,16,13]{1,2,0:T(8,128)(2,1)}), bf16[8,16,13]{1,2,0:T(8,128)(2,1)S(1)}, u32[]{:S(2)}, u32[]{:S(2)}) async-start(bf16[8,16,13]{1,2,0:T(8,128)(2,1)} %copy.127), calls=%async_computation.1 | async-start | bytes 65536 | tf_op jit(solution)/shard_map/all_to_all | solution.py:181
  22.0 0.8 slice_bitcast_fusion.1
  22.9 0.1 mul.61
  23.0 0.2 broadcast_dynamic-update-slice_fusion.3
  23.1 0.2 broadcast_dynamic-update-slice_fusion.2
  23.3 0.2 broadcast_dynamic-update-slice_fusion.1
  23.5 0.2 broadcast_dynamic-update-slice_fusion.w_ref
  23.7 0.2 copy.116
  23.8 0.1 concatenate.49
  23.9 0.3 reshape.167.ids
  24.2 0.1 add.172
  24.3 0.2 copy.120
  24.5 0.1 add.180
  24.6 0.0 collective-permute-done.9
  24.6 3.9 %collective-permute-start.7 = (s32[1,8,12,8]{2,1,0,3:T(8,128)S(1)}, s32[1,8,12,8]{2,1,0,3:T(8,128)S(1)}, u32[]{:S(2)}, u32[]{:S(2)}) collective-permute-start(s32[1,8,12,8]{2,1,0,3:T(8,128)S(1)} %get-tuple-element.27), channel_id=1, source_target_pairs={{0,24},{8,0},{16,8},{24,16},{1,25},{9,1},{17,9},{25,17},{2,26},{10... | collective-permute-start | bytes 9224 | tf_op jit(solution)/shard_map/ppermute | solution.py:130
  28.5 0.1 copy.117
  28.5 0.1 concatenate.50
  28.6 0.0 collective-permute-done.8
  28.6 0.1 collective-permute-start.11
  28.7 0.1 copy.115
  28.8 0.1 concatenate.48
  28.9 0.9 collective-permute-done.11
  29.9 0.2 collective-permute-start.10
  30.1 0.1 pad_add_fusion.1
  30.1 0.9 collective-permute-done.10
  31.1 0.1 select_add_fusion
  31.2 13.7 %collective-permute-done.7 = s32[1,8,12,8]{2,1,0,3:T(8,128)S(1)} collective-permute-done((s32[1,8,12,8]{2,1,0,3:T(8,128)S(1)}, s32[1,8,12,8]{2,1,0,3:T(8,128)S(1)}, u32[]{:S(2)}, u32[]{:S(2)}) %collective-permute-start.7) | collective-permute-done | bytes 3104 | tf_op jit(solution)/shard_map/ppermute | solution.py:130
  44.8 1.2 collective-permute-done.6
  46.1 0.1 add_add_fusion
  46.2 0.2 copy.112
  46.3 0.1 add.170
  46.5 0.2 copy.111
  46.6 0.1 concatenate.46
  46.7 1.5 %collective-permute-start.1 = (bf16[2,1,12,8,512]{4,1,2,0,3:T(2,128)(2,1)}, bf16[2,1,12,8,512]{4,1,2,0,3:T(2,128)(2,1)S(1)}, u32[]{:S(2)}, u32[]{:S(2)}) collective-permute-start(bf16[2,1,12,8,512]{4,1,2,0,3:T(2,128)(2,1)} %get-tuple-element.16), channel_id=1, source_target_pairs={{0,2},{2,4},{4,6},{6,0},{1,3},{3,5},{5,7},{7,1},{8,10},{10,12},{12... | collective-permute-start | bytes 589832 | tf_op jit(solution)/shard_map/ppermute | solution.py:130
  48.3 0.1 pad_add_fusion.xk
  48.4 1.0 fusion.6
  49.4 0.2 copy.108
  49.5 9.9 %collective-permute-done.1 = bf16[2,1,12,8,512]{4,1,2,0,3:T(2,128)(2,1)S(1)} collective-permute-done((bf16[2,1,12,8,512]{4,1,2,0,3:T(2,128)(2,1)}, bf16[2,1,12,8,512]{4,1,2,0,3:T(2,128)(2,1)S(1)}, u32[]{:S(2)}, u32[]{:S(2)}) %collective-permute-start.1) | collective-permute-done | bytes 196640 | tf_op jit(solution)/shard_map/ppermute | solution.py:130
  59.4 4.7 %fusion.2 = bf16[4,10,12,8,512]{4,1,2,0,3:T(8,128)(2,1)S(1)} fusion(bf16[1,8,12,8,512]{4,1,2,0,3:T(8,128)(2,1)} %collective-permute-done.3, bf16[1,8,12,8,512]{4,1,2,0,3:T(8,128)(2,1)} %collective-permute-done, bf16[2,1,12,8,512]{4,1,2,0,3:T(2,128)(2,1)} %collective-permute-done.2, bf16[2,8,12,8,512]{4,1,2,0,3:T(8,128)(2,1)S(1)} %bitcast.49, ...), kind=kLoop, calls=%fused_computation.4 | loop fusion | flops 27525120 | bytes 7471104 | tf_op jit(solution)/shard_map/concatenate | solution.py:151
  64.1 2.2 %copy.139 = bf16[4,10,12,8,512]{4,3,2,1,0:T(8,128)(2,1)S(1)} copy(bf16[4,10,12,8,512]{4,1,2,0,3:T(8,128)(2,1)S(1)} %fusion.2) | data formatting | bytes 7864320 | tf_op jit(solution)/shard_map/concatenate | solution.py:151
  66.4 0.1 broadcast_in_dim.22.coef
  66.4 14.8 %transport_relax.1 = bf16[8,12,16,512]{3,2,1,0:T(8,128)(2,1)} custom-call(bf16[4,10,96,512]{3,2,1,0:T(8,128)(2,1)S(1)} %bitcast.43, bf16[16,32,512]{2,1,0:T(8,128)(2,1)S(1)} %bitcast.44, s32[16,1,192]{2,1,0:T(1,128)S(1)} %pad_add_fusion.xk, s32[16,1,192]{2,1,0:T(1,128)S(1)} %reshape.158.yk, s32[16,1,128]{2,1,0:T(1,128)S(1)} %bitcast.45, ...), custom_call_target="tpu_custom_call" | custom-call | tf_op jit(solution)/shard_map/transport_relax/pallas_call | solution.py:184
  81.2 5.1 %all-to-all-start = ((bf16[8,12,16,512]{3,2,1,0:T(8,128)(2,1)}), bf16[8,12,16,512]{3,2,1,0:T(8,128)(2,1)S(1)}, u32[]{:S(2)}, u32[]{:S(2)}) async-start(bf16[8,12,16,512]{3,2,1,0:T(8,128)(2,1)} %transport_relax.1), calls=%async_computation | async-start | bytes 3145728 | tf_op jit(solution)/shard_map/all_to_all | solution.py:193
  86.3 0.1 reshape.166
  86.4 0.6 copy.129
  87.0 0.5 slice_bitcast_fusion.5
  87.5 36.6 %all-to-all-done = bf16[8,12,16,512]{3,2,1,0:T(8,128)(2,1)S(1)} async-done(((bf16[8,12,16,512]{3,2,1,0:T(8,128)(2,1)}), bf16[8,12,16,512]{3,2,1,0:T(8,128)(2,1)S(1)}, u32[]{:S(2)}, u32[]{:S(2)}) %all-to-all-start) | async-done | bytes 1572896 | tf_op jit(solution)/shard_map/all_to_all | solution.py:193
  124.1 1.3 %copy.125 = bf16[8,16,12,512]{3,1,0,2:T(8,128)(2,1)} copy(bf16[8,16,12,512]{3,1,2,0:T(8,128)(2,1)S(1)} %bitcast.50) | data formatting | bytes 3145728 | tf_op jit(solution)/shard_map/transpose | solution.py:194
  (41 shorter events, 0.2 us)
Async XLA Ops:
  0.6 12.7 %copy-start.1 = (s32[2,8,8]{2,1,0:T(8,128)S(1)}, s32[2,8,8]{2,1,0:T(8,128)}, u32[]{:S(2)}) copy-start(s32[2,8,8]{2,1,0:T(8,128)} %param.7) | copy-start | bytes 1540
  0.6 12.7 %copy-start = (s32[2,8,8,12]{3,2,1,0:T(8,128)S(1)}, s32[2,8,8,12]{3,2,1,0:T(8,128)}, u32[]{:S(2)}) copy-start(s32[2,8,8,12]{3,2,1,0:T(8,128)} %param.6) | copy-start | bytes 18436
  0.7 15.0 %copy-start.2 = (s32[2,8,8]{2,1,0:T(8,128)S(1)}, s32[2,8,8]{2,1,0:T(8,128)}, u32[]{:S(2)}) copy-start(s32[2,8,8]{2,1,0:T(8,128)} %param.8) | copy-start | bytes 1540
  0.7 22.2 %copy-start.3 = (bf16[2,8,8]{2,1,0:T(8,128)(2,1)S(1)}, bf16[2,8,8]{2,1,0:T(8,128)(2,1)}, u32[]{:S(2)}) copy-start(bf16[2,8,8]{2,1,0:T(8,128)(2,1)} %param.9) | copy-start | bytes 772
  4.3 55.2 %collective-permute-start.3 = (bf16[1,8,12,8,512]{4,1,2,0,3:T(8,128)(2,1)}, bf16[1,8,12,8,512]{4,1,2,0,3:T(8,128)(2,1)}, u32[]{:S(2)}, u32[]{:S(2)}) collective-permute-start(bf16[1,8,12,8,512]{4,1,2,0,3:T(8,128)(2,1)} %get-tuple-element.19), channel_id=1, source_target_pairs={{0,24},{8,0},{16,8},{24,16},{1,25},{9,1},{17,9},{25,17},{2,26},{10... | collective-permute-start | bytes 2359304 | tf_op jit(solution)/shard_map/ppermute | solution.py:130
  9.3 50.1 %collective-permute-start = (bf16[1,8,12,8,512]{4,1,2,0,3:T(8,128)(2,1)}, bf16[1,8,12,8,512]{4,1,2,0,3:T(8,128)(2,1)}, u32[]{:S(2)}, u32[]{:S(2)}) collective-permute-start(bf16[1,8,12,8,512]{4,1,2,0,3:T(8,128)(2,1)} %get-tuple-element.18), channel_id=1, source_target_pairs={{0,8},{8,16},{16,24},{24,0},{1,9},{9,17},{17,25},{25,1},{2,10},{10... | collective-permute-start | bytes 2359304 | tf_op jit(solution)/shard_map/ppermute | solution.py:130
  10.9 38.7 %collective-permute-start.2 = (bf16[2,1,12,8,512]{4,1,2,0,3:T(2,128)(2,1)}, bf16[2,1,12,8,512]{4,1,2,0,3:T(2,128)(2,1)}, u32[]{:S(2)}, u32[]{:S(2)}) collective-permute-start(bf16[2,1,12,8,512]{4,1,2,0,3:T(2,128)(2,1)} %get-tuple-element.17), channel_id=1, source_target_pairs={{0,6},{2,0},{4,2},{6,4},{1,7},{3,1},{5,3},{7,5},{8,14},{10,8},{12,... | collective-permute-start | bytes 589832 | tf_op jit(solution)/shard_map/ppermute | solution.py:130
  13.5 11.1 %collective-permute-start.9 = (s32[2,1,12,8]{2,1,0,3:T(1,128)S(1)}, s32[2,1,12,8]{2,1,0,3:T(1,128)S(1)}, u32[]{:S(2)}, u32[]{:S(2)}) collective-permute-start(s32[2,1,12,8]{2,1,0,3:T(1,128)S(1)} %get-tuple-element.25), channel_id=1, source_target_pairs={{0,6},{2,0},{4,2},{6,4},{1,7},{3,1},{5,3},{7,5},{8,14},{10,8},{12,... | collective-permute-start | bytes 2312 | tf_op jit(solution)/shard_map/ppermute | solution.py:130
  14.1 14.5 %collective-permute-start.8 = (s32[2,1,12,8]{2,1,0,3:T(1,128)S(1)}, s32[2,1,12,8]{2,1,0,3:T(1,128)S(1)}, u32[]{:S(2)}, u32[]{:S(2)}) collective-permute-start(s32[2,1,12,8]{2,1,0,3:T(1,128)S(1)} %get-tuple-element.24), channel_id=1, source_target_pairs={{0,2},{2,4},{4,6},{6,0},{1,3},{3,5},{5,7},{7,1},{8,10},{10,12},{12... | collective-permute-start | bytes 2312 | tf_op jit(solution)/shard_map/ppermute | solution.py:130
  16.9 64.3 %all-to-all-start.1 = ((bf16[8,16,13]{1,2,0:T(8,128)(2,1)}), bf16[8,16,13]{1,2,0:T(8,128)(2,1)S(1)}, u32[]{:S(2)}, u32[]{:S(2)}) async-start(bf16[8,16,13]{1,2,0:T(8,128)(2,1)} %copy.127), calls=%async_computation.1 | async-start | bytes 65536 | tf_op jit(solution)/shard_map/all_to_all | solution.py:181
  24.6 20.2 %collective-permute-start.7 = (s32[1,8,12,8]{2,1,0,3:T(8,128)S(1)}, s32[1,8,12,8]{2,1,0,3:T(8,128)S(1)}, u32[]{:S(2)}, u32[]{:S(2)}) collective-permute-start(s32[1,8,12,8]{2,1,0,3:T(8,128)S(1)} %get-tuple-element.27), channel_id=1, source_target_pairs={{0,24},{8,0},{16,8},{24,16},{1,25},{9,1},{17,9},{25,17},{2,26},{10... | collective-permute-start | bytes 9224 | tf_op jit(solution)/shard_map/ppermute | solution.py:130
  28.6 1.2 collective-permute-start.11
  29.9 1.2 collective-permute-start.10
  31.1 15.0 %collective-permute-start.6 = (s32[1,8,12,8]{2,1,0,3:T(8,128)S(1)}, s32[1,8,12,8]{2,1,0,3:T(8,128)S(1)}, u32[]{:S(2)}, u32[]{:S(2)}) collective-permute-start(s32[1,8,12,8]{2,1,0,3:T(8,128)S(1)} %get-tuple-element.26), channel_id=1, source_target_pairs={{0,8},{8,16},{16,24},{24,0},{1,9},{9,17},{17,25},{25,1},{2,10},{10... | collective-permute-start | bytes 9224 | tf_op jit(solution)/shard_map/ppermute | solution.py:130
  44.8 1.9 %collective-permute-start.5 = (bf16[2,8,12,512]{3,1,2,0:T(8,128)(2,1)}, bf16[2,8,12,512]{3,1,2,0:T(8,128)(2,1)S(1)}, u32[]{:S(2)}, u32[]{:S(2)}) collective-permute-start(bf16[2,8,12,512]{3,1,2,0:T(8,128)(2,1)} %get-tuple-element.15), channel_id=1, source_target_pairs={{0,1},{1,0},{2,3},{3,2},{4,5},{5,4},{6,7},{7,6},{8,9},{9,8},{10,11... | collective-permute-start | bytes 589832 | tf_op jit(solution)/shard_map/ppermute | solution.py:130
  46.1 2.3 %collective-permute-start.4 = (bf16[2,8,12,512]{3,1,2,0:T(8,128)(2,1)}, bf16[2,8,12,512]{3,1,2,0:T(8,128)(2,1)}, u32[]{:S(2)}, u32[]{:S(2)}) collective-permute-start(bf16[2,8,12,512]{3,1,2,0:T(8,128)(2,1)} %get-tuple-element.14), channel_id=1, source_target_pairs={{0,1},{1,0},{2,3},{3,2},{4,5},{5,4},{6,7},{7,6},{8,9},{9,8},{10,11... | collective-permute-start | bytes 589832 | tf_op jit(solution)/shard_map/ppermute | solution.py:130
  46.7 12.7 %collective-permute-start.1 = (bf16[2,1,12,8,512]{4,1,2,0,3:T(2,128)(2,1)}, bf16[2,1,12,8,512]{4,1,2,0,3:T(2,128)(2,1)S(1)}, u32[]{:S(2)}, u32[]{:S(2)}) collective-permute-start(bf16[2,1,12,8,512]{4,1,2,0,3:T(2,128)(2,1)} %get-tuple-element.16), channel_id=1, source_target_pairs={{0,2},{2,4},{4,6},{6,0},{1,3},{3,5},{5,7},{7,1},{8,10},{10,12},{12... | collective-permute-start | bytes 589832 | tf_op jit(solution)/shard_map/ppermute | solution.py:130
  81.2 42.9 %all-to-all-start = ((bf16[8,12,16,512]{3,2,1,0:T(8,128)(2,1)}), bf16[8,12,16,512]{3,2,1,0:T(8,128)(2,1)S(1)}, u32[]{:S(2)}, u32[]{:S(2)}) async-start(bf16[8,12,16,512]{3,2,1,0:T(8,128)(2,1)} %transport_relax.1), calls=%async_computation | async-start | bytes 3145728 | tf_op jit(solution)/shard_map/all_to_all | solution.py:193

commit v2 on v1

v2 whole, which is shorter than its diff:
```python
import functools
import math

import jax
import jax.numpy as jnp
from jax import lax
from jax.experimental import pallas as pl
from jax.experimental.pallas import tpu as pltpu
from jax.sharding import PartitionSpec as P

NV1 = 48
BLK = 8
EDGE = NV1 // BLK
STEP_COEFF = 0.6
IMPACT_KIND = 0.02
ZPAD = 16
XPARTS = 4
PARTS = 4


def weights():
    j = jnp.arange(BLK**3, dtype=jnp.int32)
    w = [c.astype(jnp.float32) - (BLK - 1) / 2.0 for c in (j // (BLK * BLK), j // BLK % BLK, j % BLK)]
    cols = [jnp.ones_like(w[0]), *w, w[0] * w[0] + w[1] * w[1] + w[2] * w[2]]
    return jnp.concatenate([jnp.broadcast_to(c[:, None], (BLK**3, 128)) for c in cols], axis=1).astype(jnp.bfloat16)


def column(slots, sz, ext_x, ext_y, own, zrows, xkeys, ykeys, own_keys, zkeys, ids, coef, w_ref):
    rows = slots * sz
    shape = (rows, 128)
    listed = jnp.broadcast_to(ids, shape)
    live = listed >= 0
    z = lax.broadcasted_iota(jnp.int32, shape, 0) % sz
    bx = (listed * 1821) >> 16
    rem = listed - bx * (EDGE * EDGE)
    by = (rem * 10923) >> 16
    bz = rem - by * EDGE
    half = EDGE // 2

    dot = functools.partial(jnp.dot, preferred_element_type=jnp.float32)

    def pick(key, others, values):
        key = jnp.where(live, key, -5)[:, :1]
        total = None
        for other, value in zip(others, values):
            hit = jnp.where(key == other[:, : value.shape[0]], 1.0, 0.0).astype(jnp.bfloat16)
            got = dot(hit, value)
            total = got if total is None else total + got
        return total

    here = listed + 256 * z
    gx = pick(here + jnp.where(bx >= half, 0, 4096), (xkeys[0], xkeys[1] + 4096), ext_x)
    gy = pick(here + jnp.where(by >= half, 0, 4096), (ykeys[0], ykeys[1] + 4096), ext_y)
    zkey = listed + 256 * jnp.where(bz >= half, z, z + 2)
    gz = pick(zkey, (own_keys + 256, *zkeys), (own, *zrows))

    offset = (BLK - 1) / 2.0 - (NV1 - 1) / 2.0
    c = [b.astype(jnp.float32) * BLK + offset for b in (bx, by, bz)]
    lane = lax.broadcasted_iota(jnp.int32, (1, 128), 1)
    mid = (BLK - 1) / 2.0
    wx = [(lane // 64 + 2 * t).astype(jnp.float32) - mid for t in range(4)]
    wy = (lane // BLK % BLK).astype(jnp.float32) - mid
    wz = (lane % BLK).astype(jnp.float32) - mid
    vy, vz = jnp.abs(c[1] + wy), jnp.abs(c[2] + wz)
    lam = STEP_COEFF / (NV1 - 1)
    reads = []
    for t in range(4):
        cut = slice(128 * t, 128 * (t + 1))
        f = own[:, cut].astype(jnp.float32)
        flux = jnp.abs(c[0] + wx[t]) * (f - gx[:, cut]) + vy * (f - gy[:, cut]) + vz * (f - gz[:, cut])
        reads.append(jnp.where(live, f - lam * flux, 0.0).astype(jnp.bfloat16))
    sums = dot(reads[0], w_ref[0:128, :])
    for t in range(1, 4):
        sums = sums + dot(reads[t], w_ref[128 * t : 128 * (t + 1), :])
    s = [sums[:, 128 * k : 128 * (k + 1)] for k in range(5)]

    def per_cell(a):
        return jnp.sum(a.reshape(slots, sz, 128), axis=0)

    mass = per_cell(s[0])
    momentum = [per_cell(s[0] * c[k] + s[1 + k]) for k in range(3)]
    sq = c[0] * c[0] + c[1] * c[1] + c[2] * c[2]
    cross = c[0] * s[1] + c[1] * s[2] + c[2] * s[3]
    energy = per_cell(s[0] * sq + 2.0 * cross + s[4])
    u = [m / mass for m in momentum]
    temperature = (energy / mass - (u[0] * u[0] + u[1] * u[1] + u[2] * u[2])) / 3.0
    target = temperature * (1.0 + coef) * (1.0 + coef) / 4.0
    rate = 1.0 - jnp.exp(-IMPACT_KIND * (mass / BLK**3) * jnp.sqrt(temperature))
    area = 2.0 * math.pi * target
    scale = mass / (area * jnp.sqrt(area))
    inv = -0.5 / target

    cube = (slots, sz, 128)
    a = [c[k].reshape(cube) - u[k][None] for k in range(3)]
    oy, oz = a[1] + wy[None], a[2] + wz[None]
    q = oy * oy + oz * oz
    live3 = listed.reshape(cube) >= 0
    outs = []
    for t in range(4):
        ox = a[0] + wx[t][None]
        maxwellian = scale[None] * jnp.exp((ox * ox + q) * inv[None])
        r = reads[t].astype(jnp.float32).reshape(cube)
        outs.append(jnp.where(live3, r + rate[None] * (maxwellian - r), 0.0))
    return outs


MESH = pl.DeviceIdType.MESH


def whole_kernel(
    sizes, f, zlast, zfirst, krow, klast, kfirst, meta, ids, coef, w_ref, pos,
    out, meta_out,
    ext, zlo, zhi, kext, kzlo, kzhi, pay, sendb, x_sem, face_sem, local_sem, move_sem, meta_sem,
):
    cx, cy, sz, slots, groups, cap, xparts, parts = sizes
    gx, gy, gz = (lax.axis_index(a) for a in ("gx", "gy", "gz"))
    nx, ny, nz = (lax.axis_size(a) for a in ("gx", "gy", "gz"))
    me = gx * nz + gz
    up_x, down_x = ((gx + 1) % nx, gy, gz), ((gx + nx - 1) % nx, gy, gz)
    up_y, down_y = (gx, (gy + 1) % ny, gz), (gx, (gy + ny - 1) % ny, gz)
    up_z, down_z = (gx, gy, (gz + 1) % nz), (gx, gy, (gz + nz - 1) % nz)

    def peer(d):
        other = (me + d) % groups
        return other // nz, gy, other % nz

    barrier = pltpu.get_barrier_semaphore()
    pl.semaphore_signal(barrier, inc=1, device_id=up_y, device_id_type=MESH)
    pl.semaphore_signal(barrier, inc=1, device_id=down_y, device_id_type=MESH)

    def greet(d, carry):
        pl.semaphore_signal(barrier, inc=1, device_id=peer(d), device_id_type=MESH)
        return carry

    lax.fori_loop(1, groups, greet, 0)

    inner = pltpu.make_async_copy(f, ext.at[pl.ds(1, cx), pl.ds(1, cy)], local_sem.at[0])
    inner.start()
    inner_keys = pltpu.make_async_copy(krow, kext.at[pl.ds(1, cx), pl.ds(1, cy)], local_sem.at[1])
    inner_keys.start()
    own_meta = pltpu.make_async_copy(meta.at[me], meta_out.at[me], local_sem.at[2])
    own_meta.start()
    pl.semaphore_wait(barrier, groups + 1)

    def remote(src, dst, sems, index, to):
        return pltpu.make_async_remote_copy(
            src_ref=src, dst_ref=dst, send_sem=sems.at[(0, *index)], recv_sem=sems.at[(1, *index)],
            device_id=to, device_id_type=MESH,
        )

    ys = pl.ds(1, cy)
    xs = pl.ds(1, cx)
    faces = [
        (krow.at[cx - 1], kext.at[0, ys], up_x),
        (krow.at[0], kext.at[cx + 1, ys], down_x),
        (krow.at[:, cy - 1], kext.at[xs, 0], up_y),
        (krow.at[:, 0], kext.at[xs, cy + 1], down_y),
        (klast, kzlo, up_z),
        (kfirst, kzhi, down_z),
        (f.at[:, cy - 1], ext.at[xs, 0], up_y),
        (f.at[:, 0], ext.at[xs, cy + 1], down_y),
        (zlast, zlo, up_z),
        (zfirst, zhi, down_z),
    ]
    faces = [remote(src, dst, face_sem, (i,), to) for i, (src, dst, to) in enumerate(faces)]
    for copy in faces:
        copy.start()

    per = cy // xparts

    def x_copies(q):
        own, there = pl.ds(q * per, per), pl.ds(1 + q * per, per)
        return (
            remote(f.at[cx - 1, own], ext.at[0, there], x_sem, (0, q), up_x),
            remote(f.at[0, own], ext.at[cx + 1, there], x_sem, (1, q), down_x),
        )

    def x_start(q, carry):
        for copy in x_copies(q):
            copy.start()
        return carry

    lax.fori_loop(0, xparts, x_start, 0)

    def meta_copy(d, row):
        return remote(meta.at[(me + d) % groups], meta_out.at[row], meta_sem, (d,), peer(d))

    def meta_start(d, carry):
        meta_copy(d, me).start()
        return carry

    lax.fori_loop(1, groups, meta_start, 0)
    inner.wait()
    inner_keys.wait()
    own_meta.wait()
    for copy in faces:
        copy.wait()

    def one(n, carry):
        y, x = n // cx, n % cx
        i = x * cy + y
        outs = column(
            slots, sz,
            (ext[x, y + 1], ext[x + 2, y + 1]),
            (ext[x + 1, y], ext[x + 1, y + 2]),
            ext[x + 1, y + 1], (zlo[i], zhi[i]),
            (kext[x, y + 1], kext[x + 2, y + 1]),
            (kext[x + 1, y], kext[x + 1, y + 2]),
            kext[x + 1, y + 1], (kzlo[i], kzhi[i]),
            ids[i], coef[i], w_ref,
        )
        for t in range(4):
            pay[:, pl.ds(pl.multiple_of(i * sz, sz), sz), 128 * t : 128 * (t + 1)] = outs[t]
        return carry

    def part(q, carry):
        for copy in x_copies(q):
            copy.wait()
        lax.fori_loop(q * per * cx, (q + 1) * per * cx, one, 0)
        return carry

    lax.fori_loop(0, xparts, part, 0)

    cells = cx * cy * sz
    perm = jnp.where(lax.broadcasted_iota(jnp.int32, (cells, cells), 0) == pos[...], 1.0, 0.0).astype(jnp.bfloat16)
    step = slots // parts

    def move_copy(p, d, row):
        cut = pl.ds(p * step, step)
        return remote(sendb.at[(me + d) % groups, cut], out.at[row, cut], move_sem, (p, d), peer(d))

    def own_copy(p):
        cut = pl.ds(p * step, step)
        return pltpu.make_async_copy(sendb.at[me, cut], out.at[me, cut], local_sem.at[3 + p])

    def send(p, carry):
        for k in range(step):
            s = p * step + k
            rows = jnp.dot(perm, pay[s].astype(jnp.bfloat16), preferred_element_type=jnp.float32)
            for g in range(groups):
                sendb[g, s] = rows[g * cap : (g + 1) * cap].astype(jnp.bfloat16)

        def start(d, inner_carry):
            move_copy(p, d, me).start()
            return inner_carry

        lax.fori_loop(1, groups, start, 0)
        own_copy(p).start()
        return carry

    lax.fori_loop(0, parts, send, 0)

    def finish(d, carry):
        source = (me + groups - d) % groups
        copy = meta_copy(d, source)
        copy.wait_send()
        copy.wait_recv()
        return carry

    lax.fori_loop(1, groups, finish, 0)

    def finish_part(p, carry):
        own_copy(p).wait()

        def finish_one(d, inner_carry):
            copy = move_copy(p, d, (me + groups - d) % groups)
            copy.wait_send()
            copy.wait_recv()
            return inner_carry

        lax.fori_loop(1, groups, finish_one, 0)
        return carry

    lax.fori_loop(0, parts, finish_part, 0)


def on_device(distribution, block_ids, cell_counts, owner, restitution):
    cx, cy, sz, slots, vb = distribution.shape
    cells, rows, columns = cx * cy * sz, slots * sz, cx * cy
    groups = lax.axis_size("gx") * lax.axis_size("gz")
    cap = cells // groups
    live = jnp.arange(slots, dtype=jnp.int32) < cell_counts[..., None]
    listed = jnp.where(live, block_ids, -1).transpose(0, 1, 3, 2)
    f = distribution.transpose(0, 1, 3, 2, 4)
    pad = ((0, 0), (0, ZPAD - slots), (0, 0))
    zlast = jnp.pad(f[:, :, :, -1].reshape(columns, slots, vb), pad)
    zfirst = jnp.pad(f[:, :, :, 0].reshape(columns, slots, vb), pad)
    f = f.reshape(cx, cy, rows, vb)

    def lanes(keys):
        return jnp.pad(keys, ((0, 0),) * (keys.ndim - 1) + ((0, -keys.shape[-1] % 128),), constant_values=-9)

    krow = lanes((listed + 256 * jnp.arange(sz, dtype=jnp.int32)).reshape(cx, cy, 1, rows))
    klast = lanes(listed[..., -1].reshape(columns, 1, slots))
    kfirst = lanes((listed[..., 0] + 256 * (sz + 1)).reshape(columns, 1, slots))
    ids = listed.reshape(columns, rows, 1)
    coef = jnp.broadcast_to(restitution.astype(jnp.float32).reshape(columns, sz, 1), (columns, sz, 128))

    owners = owner.reshape(cells)
    order = jnp.arange(cells, dtype=jnp.int32)
    same = (owners[:, None] == owners[None, :]) & (order[:, None] < order[None, :])
    pos = owners * cap + jnp.sum(same.astype(jnp.int32), axis=0)

    meta = jnp.concatenate([block_ids.reshape(cells, slots), cell_counts.reshape(cells, 1)], axis=1)
    onehot = (order[:, None] == pos[None, :]).astype(jnp.bfloat16)
    meta = jnp.pad(meta.astype(jnp.bfloat16), ((0, 0), (0, 127 - slots)))
    meta = jnp.dot(onehot, meta, preferred_element_type=jnp.float32).astype(jnp.bfloat16)

    xparts = math.gcd(cy, XPARTS)
    parts = math.gcd(slots, PARTS)
    vmem, anywhere = pl.BlockSpec(memory_space=pltpu.VMEM), pl.BlockSpec(memory_space=pl.ANY)
    bf16, i32 = jnp.bfloat16, jnp.int32
    received, meta = pl.pallas_call(
        functools.partial(whole_kernel, (cx, cy, sz, slots, groups, cap, xparts, parts)),
        out_shape=(
            jax.ShapeDtypeStruct((groups, slots, cap, vb), bf16),
            jax.ShapeDtypeStruct((groups, cap, 128), bf16),
        ),
        in_specs=[anywhere] * 3 + [vmem] * 8,
        out_specs=(anywhere, anywhere),
        scratch_shapes=[
            pltpu.VMEM((cx + 2, cy + 2, rows, vb), bf16),
            pltpu.VMEM((columns, ZPAD, vb), bf16),
            pltpu.VMEM((columns, ZPAD, vb), bf16),
            pltpu.VMEM((cx + 2, cy + 2, 1, krow.shape[-1]), i32),
            pltpu.VMEM((columns, 1, 128), i32),
            pltpu.VMEM((columns, 1, 128), i32),
            pltpu.VMEM((slots, cells, vb), jnp.float32),
            pltpu.VMEM((groups, slots, cap, vb), bf16),
            pltpu.SemaphoreType.DMA((2, 2, xparts)),
            pltpu.SemaphoreType.DMA((2, 10)),
            pltpu.SemaphoreType.DMA((3 + parts,)),
            pltpu.SemaphoreType.DMA((2, parts, groups)),
            pltpu.SemaphoreType.DMA((2, groups)),
        ],
        compiler_params=pltpu.CompilerParams(
            collective_id=0, has_side_effects=True, vmem_limit_bytes=48 << 20
        ),
        name="transport_relax_move",
    )(f, zlast, zfirst, krow, klast, kfirst, meta.reshape(groups, cap, 128), ids, coef, weights(), pos.reshape(1, cells))
    moved = received.transpose(0, 2, 1, 3).reshape(1, cells, slots, vb)
    meta = meta.reshape(cells, 128)[:, : slots + 1].astype(i32)
    return moved, meta[:, :slots].reshape(1, cells, slots), meta[:, slots].reshape(1, cells)


def solution(mesh):
    placed = (
        P("gx", "gy", "gz", None, None),
        P("gx", "gy", "gz", None),
        P("gx", "gy", "gz"),
        P("gx", "gy", "gz"),
        P("gx", "gy", "gz"),
    )
    return jax.shard_map(
        on_device,
        mesh=mesh,
        in_specs=placed,
        out_specs=(
            P("gy", ("gx", "gz"), None, None),
            P("gy", ("gx", "gz"), None),
            P("gy", ("gx", "gz")),
        ),
        check_vma=False,
    )
```

time: 126 us -> 90.9 us (0.72)
  Pallas kernels: 14.8 us -> 79.2 us
  waiting for transfers between devices: 63.3 us -> 0 us
  starting transfers between devices: 25.4 us -> 0 us
  local copies, waits for them, and re-layouts: 14.5 us -> 6.3 us
  other arithmetic: 6.27 us -> 4.06 us
    pallas_call x1, Pallas kernels: 14.8 us -> 79.2 us  [on_device(): pl.pallas_call(functools.partial(whole_kernel, (cx, cy, sz, slots, groups...]
    all_to_all x2 -> x0, waiting for transfers between devices: 36.6 us -> none  [the longest x1 36.6 us: on_device(): lax.all_to_all(outgoing, ('gx', 'gz'), split_axis=0, concat_axis=0, tiled...]
    ppermute x12 -> x0, waiting for transfers between devices: 26.7 us -> none  [shifted(): lax.ppermute(value, axis, [(i, (i + step) % peers) for i in range(peers)])]
    ppermute x12 -> x0, starting transfers between devices: 15.2 us -> none  [shifted(): lax.ppermute(value, axis, [(i, (i + step) % peers) for i in range(peers)])]
    all_to_all x2 -> x0, starting transfers between devices: 10.1 us -> none  [the longest x1 5.1 us: on_device(): lax.all_to_all(meta, ('gx', 'gz'), split_axis=0, concat_axis=0, tiled=True)]
    concatenate x5 -> x0, other arithmetic: 5.88 us -> none  [the longest x1 4.67 us: on_device(): jnp.concatenate([jnp.pad(xlo, wide), middle, jnp.pad(xhi, wide)], axis=0)]
    slice x5 -> x0, local copies, waits for them, and re-layouts: 3.01 us -> none  [the longest x1 1.53 us: on_device(): ylo, yhi = (shifted(f[:, -1:], 'gy', 1), shifted(f[:, :1], 'gy', -1))]
    concatenate x6 -> x0, local copies, waits for them, and re-layouts: 2.78 us -> none  [the longest x1 2.23 us: on_device(): jnp.concatenate([jnp.pad(xlo, wide), middle, jnp.pad(xhi, wide)], axis=0)]
  transfers between devices with their start and end apart: 14 -> 0, of which waited for: 6 -> 0; matrix products, arithmetic and copies ran while one was open for 13% -> 0% of each run, Pallas kernels for 12% -> 0%
where the time goes in v2:
time: 90.9 us; the launch traced here: 90.6 us
  Pallas kernels  79.2 us (87%)
  local copies, waits for them, and re-layouts  6.3 us (7%)
  other arithmetic  4.06 us (4%)
    pallas_call x1, Pallas kernels, on_device(): pl.pallas_call(functools.partial(whole_kernel, (cx, cy, sz, slots, groups...  79.2 us

profile of v2, /device:TPU:0, one launch (start us, length us, event | category | flops | bytes accessed | tf_op | source)
XLA Modules:
  0.0 90.6 jit_solution(5395649977939592142)
XLA Ops:
  0.6 0.0 copy-start
  0.6 0.9 reshape.142
  1.5 0.1 convert_reduce_fusion
  1.7 0.7 convert.28
  2.4 0.1 reshape.144
  2.5 0.7 bitcast_convert_fusion
  3.2 0.7 broadcast_multiply_fusion
  3.9 0.1 mul.57
  4.0 0.8 convert.27
  4.9 0.1 copy.67
  4.9 0.2 convolution_convert_fusion
  5.1 0.1 broadcast_in_dim.22.coef
  5.2 0.9 %broadcast_add_fusion = (s32[2,8,12,8]{2,3,1,0:T(8,128)S(1)}, s32[2,8,12,8]{2,3,1,0:T(8,128)S(1)}) fusion(s32[8]{0:T(128)S(1)} %iota_multiply_fusion, s32[2,8,8,12]{3,2,1,0:T(8,128)} %param.6, s32[2,8,8]{2,1,0:T(8,128)} %param.7), kind=kLoop, calls=%fused_computation.23 | loop fusion | flops 4608 | bytes 18976 | tf_op jit(solution)/shard_map/add | solution.py:293
  6.2 0.2 copy.60
  6.3 0.2 copy.57
  6.5 0.1 reshape.141
  6.6 0.2 reshape.151.ids
  6.9 0.2 broadcast_dynamic-update-slice_fusion.3
  7.1 0.2 broadcast_dynamic-update-slice_fusion.2
  7.3 0.2 broadcast_dynamic-update-slice_fusion.1
  7.4 0.2 broadcast_dynamic-update-slice_fusion.w_ref
  7.6 0.0 copy-done
  7.6 0.9 copy.71
  8.5 0.1 copy.56
  8.7 0.1 copy.55
  8.8 79.2 %transport_relax_move.1 = (bf16[8,12,16,512]{3,2,1,0:T(8,128)(2,1)S(1)}, bf16[8,16,128]{2,1,0:T(8,128)(2,1)S(1)}) custom-call(bf16[2,8,96,512]{3,2,1,0:T(8,128)(2,1)S(1)} %bitcast.32, bf16[16,16,512]{2,1,0:T(8,128)(2,1)S(1)} %pad.22.zlast, bf16[16,16,512]{2,1,0:T(8,128)(2,1)S(1)} %pad.23.zfirst, s32[2,8,1,128]{3,2,1,0:T(1,128)S(1)} %pad.24.krow, ...), custom_call_target="tpu_custom_call" | custom-call | tf_op jit(solution)/shard_map/transport_relax_move/pallas_call | solution.py:313
  88.1 1.3 %copy.64 = bf16[8,16,12,512]{3,1,0,2:T(8,128)(2,1)} copy(bf16[8,16,12,512]{3,1,2,0:T(8,128)(2,1)S(1)} %bitcast.33) | data formatting | bytes 3145728 | tf_op jit(solution)/shard_map/transpose | solution.py:341
  89.4 0.1 copy.69
  89.4 0.6 slice_bitcast_fusion.2
  90.0 0.6 reshape.149
  (16 shorter events, 0.2 us)
Async XLA Ops:
  0.6 7.0 %copy-start = (bf16[2,8,8,12,512]{4,2,3,1,0:T(8,128)(2,1)S(1)}, bf16[2,8,8,12,512]{4,2,3,1,0:T(8,128)(2,1)}, u32[]{:S(2)}) copy-start(bf16[2,8,8,12,512]{4,2,3,1,0:T(8,128)(2,1)} %param.5) | copy-start | bytes 4718596

commit v3 on v2

--- a/solution.py
+++ b/solution.py
@@ -3,6 +3,8 @@
 
 import jax
 import jax.numpy as jnp
+import ml_dtypes
+import numpy as np
 from jax import lax
 from jax.experimental import pallas as pl
 from jax.experimental.pallas import tpu as pltpu
@@ -14,15 +16,16 @@
 STEP_COEFF = 0.6
 IMPACT_KIND = 0.02
 ZPAD = 16
-XPARTS = 4
+XPARTS = 8
+WINDOW = 3
 PARTS = 4
 
 
 def weights():
-    j = jnp.arange(BLK**3, dtype=jnp.int32)
-    w = [c.astype(jnp.float32) - (BLK - 1) / 2.0 for c in (j // (BLK * BLK), j // BLK % BLK, j % BLK)]
-    cols = [jnp.ones_like(w[0]), *w, w[0] * w[0] + w[1] * w[1] + w[2] * w[2]]
-    return jnp.concatenate([jnp.broadcast_to(c[:, None], (BLK**3, 128)) for c in cols], axis=1).astype(jnp.bfloat16)
+    j = np.arange(BLK**3)
+    w = [c - (BLK - 1) / 2.0 for c in (j // (BLK * BLK), j // BLK % BLK, j % BLK)]
+    cols = [np.ones(BLK**3), *w, w[0] * w[0] + w[1] * w[1] + w[2] * w[2]]
+    return np.repeat(np.stack(cols, axis=1), 128, axis=1).astype(ml_dtypes.bfloat16)
 
 
 def column(slots, sz, ext_x, ext_y, own, zrows, xkeys, ykeys, own_keys, zkeys, ids, coef, w_ref):
@@ -180,7 +183,7 @@
             copy.start()
         return carry
 
-    lax.fori_loop(0, xparts, x_start, 0)
+    lax.fori_loop(0, min(WINDOW, xparts), x_start, 0)
 
     def meta_copy(d, row):
         return remote(meta.at[(me + d) % groups], meta_out.at[row], meta_sem, (d,), peer(d))
@@ -216,6 +219,11 @@
     def part(q, carry):
         for copy in x_copies(q):
             copy.wait()
+
+        @pl.when(q + WINDOW < xparts)
+        def _():
+            x_start(q + WINDOW, 0)
+
         lax.fori_loop(q * per * cx, (q + 1) * per * cx, one, 0)
         return carry
 
@@ -337,7 +345,7 @@
             collective_id=0, has_side_effects=True, vmem_limit_bytes=48 << 20
         ),
         name="transport_relax_move",
-    )(f, zlast, zfirst, krow, klast, kfirst, meta.reshape(groups, cap, 128), ids, coef, weights(), pos.reshape(1, cells))
+    )(f, zlast, zfirst, krow, klast, kfirst, meta.reshape(groups, cap, 128), ids, coef, jnp.asarray(weights()), pos.reshape(1, cells))
     moved = received.transpose(0, 2, 1, 3).reshape(1, cells, slots, vb)
     meta = meta.reshape(cells, 128)[:, : slots + 1].astype(i32)
     return moved, meta[:, :slots].reshape(1, cells, slots), meta[:, slots].reshape(1, cells)

time: 90.9 us -> 99.1 us (1.090)
  local copies, waits for them, and re-layouts: 6.3 us -> 14.5 us
  Pallas kernels: 79.2 us -> 77.8 us
    unnamed x8 -> x16, local copies, waits for them, and re-layouts: 1.43 us -> 4.86 us
    add x1, local copies, waits for them, and re-layouts: 0.17 us -> 1.66 us  [on_device(): listed + 256 * jnp.arange(sz, dtype=jnp.int32)]
    reshape x1, local copies, waits for them, and re-layouts: 0.11 us -> 1.59 us  [on_device(): (listed + 256 * jnp.arange(sz, dtype=jnp.int32)).reshape(cx, cy, 1, rows)]
    pallas_call x1, Pallas kernels: 79.2 us -> 77.8 us  [on_device(): pl.pallas_call(functools.partial(whole_kernel, (cx, cy, sz, slots, groups...]
    transpose x1, local copies, waits for them, and re-layouts: 1.31 us -> 2.71 us  [on_device(): moved = received.transpose(0, 2, 1, 3).reshape(1, cells, slots, vb)]
where the time goes in v3:
time: 99.1 us; the launch traced here: 98.5 us
  Pallas kernels  77.8 us (79%)
  local copies, waits for them, and re-layouts  14.5 us (15%)
  other arithmetic  4.62 us (5%)
    pallas_call x1, Pallas kernels, on_device(): pl.pallas_call(functools.partial(whole_kernel, (cx, cy, sz, slots, groups...  77.8 us
    unnamed x16, local copies, waits for them, and re-layouts  4.86 us
    transpose x1, local copies, waits for them, and re-layouts, on_device(): moved = received.transpose(0, 2, 1, 3).reshape(1, cells, slots, vb)  2.71 us

profile of v3, /device:TPU:0, one launch (start us, length us, event | category | flops | bytes accessed | tf_op | source)
XLA Modules:
  0.0 98.5 jit_solution(1257529358269622566)
XLA Ops:
  0.6 0.0 copy-start.6
  0.6 0.0 copy-start
  0.7 1.7 %broadcast_add_fusion = (s32[2,8,12,8]{2,3,1,0:T(8,128)}, s32[2,8,12,8]{2,3,1,0:T(8,128)S(1)}) fusion(s32[8]{0:T(128)S(1)} %iota_multiply_fusion, s32[2,8,8,12]{3,2,1,0:T(8,128)} %param.7, s32[2,8,8]{2,1,0:T(8,128)} %param.8), kind=kLoop, calls=%fused_computation.18 | loop fusion | flops 4608 | bytes 18976 | tf_op jit(solution)/shard_map/add | solution.py:301
  2.4 0.8 reshape.83
  3.2 0.1 convert_reduce_fusion
  3.3 0.8 convert.9
  4.1 0.1 copy.68
  4.2 0.7 convert.10
  4.9 0.1 reshape.85
  5.0 0.8 convolution_convert_fusion
  5.8 0.2 copy.61
  6.0 0.3 reshape.92.ids
  6.2 0.0 copy-done.6
  6.2 0.1 mul.33
  6.3 0.5 bitcast_add_fusion.pos
  6.9 0.0 copy-done
  6.9 0.9 copy.72
  7.7 0.0 copy-start.2
  7.8 0.1 copy.56
  7.9 0.1 copy.57
  8.1 1.7 %copy.58 = s32[2,8,12,8]{3,2,1,0:T(8,128)} copy(s32[2,8,12,8]{2,3,1,0:T(8,128)} %get-tuple-element.7) | data formatting | bytes 12288 | tf_op jit(solution)/shard_map/add | solution.py:301
  9.8 1.6 %reshape.82 = s32[2,8,1,96]{3,1,0,2:T(8,128)} reshape(s32[2,8,12,8]{3,2,1,0:T(8,128)} %copy.58) | data formatting | bytes 12288 | tf_op jit(solution)/shard_map/reshape | solution.py:301
  11.3 0.7 pad.24.krow
  12.1 0.7 bitcast_convert_fusion
  12.7 0.1 broadcast_in_dim.24.coef
  12.8 0.0 copy-done.2
  12.8 0.0 copy-start.3
  12.8 0.8 copy-done.3
  13.6 0.0 copy-start.5
  13.6 0.7 copy-done.5
  14.2 77.8 %transport_relax_move.1 = (bf16[8,12,16,512]{3,2,1,0:T(8,128)(2,1)S(1)}, bf16[8,16,128]{2,1,0:T(8,128)(2,1)S(1)}) custom-call(bf16[2,8,96,512]{3,2,1,0:T(8,128)(2,1)S(1)} %bitcast.32, bf16[16,16,512]{2,1,0:T(8,128)(2,1)S(1)} %pad.22.zlast, bf16[16,16,512]{2,1,0:T(8,128)(2,1)S(1)} %pad.23.zfirst, s32[2,8,1,128]{3,2,1,0:T(1,128)S(1)} %pad.24.krow, ...), custom_call_target="tpu_custom_call" | custom-call | tf_op jit(solution)/shard_map/transport_relax_move/pallas_call | solution.py:321
  92.1 0.0 copy-start.1
  92.1 1.1 %copy-done.1 = bf16[8,12,16,512]{3,2,1,0:T(8,128)(2,1)} copy-done((bf16[8,12,16,512]{3,2,1,0:T(8,128)(2,1)}, bf16[8,12,16,512]{3,2,1,0:T(8,128)(2,1)S(1)}, u32[]{:S(2)}) %copy-start.1) | copy-done | bytes 1572888
  93.2 0.0 copy-start.4
  93.2 0.6 copy-done.4
  93.8 0.8 copy.70
  94.7 0.6 reshape.90
  95.3 0.5 slice_bitcast_fusion.2
  95.8 2.7 %copy.65 = bf16[8,16,12,512]{3,1,0,2:T(8,128)(2,1)} copy(bf16[8,16,12,512]{3,1,2,0:T(8,128)(2,1)} %bitcast.33) | data formatting | bytes 3145728 | tf_op jit(solution)/shard_map/transpose | solution.py:349
  (10 shorter events, 0.1 us)
Async XLA Ops:
  0.6 5.6 %copy-start.6 = (s32[2,8,8]{2,1,0:T(8,128)S(1)}, s32[2,8,8]{2,1,0:T(8,128)}, u32[]{:S(2)}) copy-start(s32[2,8,8]{2,1,0:T(8,128)} %param.9) | copy-start | bytes 1540
  0.6 6.2 %copy-start = (bf16[2,8,8,12,512]{4,2,3,1,0:T(8,128)(2,1)S(1)}, bf16[2,8,8,12,512]{4,2,3,1,0:T(8,128)(2,1)}, u32[]{:S(2)}) copy-start(bf16[2,8,8,12,512]{4,2,3,1,0:T(8,128)(2,1)} %param.6) | copy-start | bytes 4718596
  7.7 5.1 %copy-start.2 = (bf16[512,640]{1,0:T(8,128)(2,1)S(1)}, bf16[512,640]{1,0:T(8,128)(2,1)}, u32[]{:S(2)}) copy-start(bf16[512,640]{1,0:T(8,128)(2,1)} %constant.16.clone.w_ref) | copy-start | bytes 1966084
  12.8 0.8 copy-start.3
  13.6 0.7 copy-start.5
  92.1 1.1 %copy-start.1 = (bf16[8,12,16,512]{3,2,1,0:T(8,128)(2,1)}, bf16[8,12,16,512]{3,2,1,0:T(8,128)(2,1)S(1)}, u32[]{:S(2)}) copy-start(bf16[8,12,16,512]{3,2,1,0:T(8,128)(2,1)S(1)} %get-tuple-element.5) | copy-start | bytes 4718596
  93.2 0.6 copy-start.4
